TPU v7x, 256 devices: a whole 4x4x8 slice. The times are simulated.
256 devices in a mesh: band: 16 (over x, y), wave: 16 (over z, core).
Axes of the slice: x: 4, y: 4, z: 8, core: 2. Of those that a mesh axis runs over, the one named last changes fastest.
Arguments:
- spectral: bfloat16 [640, 1408, 8], P('wave', 'band'), may hold values from -0.119628906 to 0.119628906
- legendre: bfloat16 [640, 1280, 1408], P('wave', 'band'), may hold values from -0.15625 to 0.15625
- slot_pair: int32 [640], replicated, may hold values from 0 to 639, each once
- quad_weight: float32 [1280], P('band'), may hold values from 0.4 to 2.5
- depart_code: int32 [1, 2, 1280, 5120], P(None, None, ('band', 'wave')), may hold values from 0 to 15
- stencil_pick: int32 [1, 2, 1280, 5120], P(None, None, ('band', 'wave')), may hold values from 0 to 15
- stencil_weight: float32 [16, 16], replicated, may hold values from -0.05 to 0.175
Outputs:
- arrival: bfloat16 [1, 4, 2, 1280, 5120], P(None, None, None, ('band', 'wave'))
- spectral_out: bfloat16 [640, 1408, 8], P('wave', 'band')
Inputs may be any that keep to these rules, and one draw needn't show every extreme that they name: A permutation: slot s holds the wavenumbers slot_pair[s] and 1279 - slot_pair[s]. Decodes to a latitude step depart_code // 4 - 2 and a longitude step depart_code % 4 - 2.
All inputs are finite; a program needn't handle non-finite values.
Results may differ from a plain program's by a relative error of at most 0.02.
Values may be sent and summed in bfloat16 or wider, within the bound.
A program may use at most 256 MiB of HBM per device.

v0:
```python
import math

import jax
import jax.numpy as jnp
from jax import lax
from jax.sharding import PartitionSpec as P

M = 1280
NLON = 5120
FIELDS = 4
LEV = 1
DR = 2
DL = 2
NSTEN = 16
RIM = 3


def extended_2(array, sides, width):
    for axis, dim in sides:
        devices, length = (lax.axis_size(axis), array.shape[dim])
        up = [(i, (i + 1) % devices) for i in range(devices - 1)]
        down = [(j, i) for i, j in up]
        last = lax.slice_in_dim(array, length - width, length, axis=dim)
        first = lax.slice_in_dim(array, 0, width, axis=dim)
        before = lax.ppermute(last, axis, up)
        after = lax.ppermute(first, axis, down)
        array = jnp.concatenate([before, array, after], axis=dim)
    return array


def row_weights(pair_ids, row_index, wavenumbers):
    low_count = wavenumbers - pair_ids[:, None]
    higher = row_index[None, :] >= low_count
    in_use = (row_index[None, :] <= wavenumbers).astype(jnp.float32)
    degree = jnp.where(higher, row_index[None, :] - low_count, row_index[None, :])
    parity_sign = 1.0 - 2.0 * (degree % 2).astype(jnp.float32)
    high_part = higher.astype(jnp.float32)
    holder = jnp.stack([1.0 - high_part, high_part], axis=-1) * in_use[..., None]
    hemisphere = jnp.stack([jnp.ones_like(parity_sign), parity_sign], axis=-1)
    return holder[..., :, None] * hemisphere[..., None, :]


def wave_factor(slot_pair, wavenumbers):
    wave_pair = jnp.stack([slot_pair, wavenumbers - 1 - slot_pair], axis=1)
    return jnp.where(wave_pair == 0, 1.0, 2.0).astype(jnp.float32)


def angle_table(slot_pair, wavenumbers, longitudes):
    row_count = slot_pair.shape[0] * 4
    row_id = jnp.arange(row_count, dtype=jnp.int32)
    pair_of_row = jnp.repeat(slot_pair, 4)
    upper = row_id // 2 % 2
    wave_of_row = jnp.where(upper == 1, wavenumbers - 1 - pair_of_row, pair_of_row)
    sine_row = (row_id % 2 == 1)[:, None]
    factor = jnp.where(wave_of_row == 0, 1.0, 2.0).astype(jnp.float32)[:, None]
    column = jnp.arange(longitudes, dtype=jnp.int32)
    residue = wave_of_row[:, None] * column[None, :] % longitudes
    angles = residue.astype(jnp.float32) * (2.0 * math.pi / longitudes)
    values = jnp.where(sine_row, -factor * jnp.sin(angles), factor * jnp.cos(angles))
    return values.astype(jnp.bfloat16)


def interpolate_window(padded, departure, tap_weight):
    levels, fields, hemispheres, padded_rows, longitudes = padded.shape
    height = padded_rows - 2 * RIM
    row_shift = departure // (2 * DL) - DR
    col_shift = departure % (2 * DL) - DL
    row_match = {}
    for value in range(-DR, DR):
        row_match[value] = row_shift == value
    col_match = {}
    for value in range(-DL, DL):
        col_match[value] = col_shift == value
    tap_values = [tap_weight(tap_index) for tap_index in range(16)]
    running = jnp.zeros((levels, fields, hemispheres, height, longitudes), jnp.float32)
    for shift_row in range(-DR - 1, DR + 2):
        row_slab = padded[:, :, :, RIM + shift_row : RIM + shift_row + height, :].astype(
            jnp.float32
        )
        for shift_col in range(-DL - 1, DL + 2):
            factor = jnp.zeros(departure.shape, jnp.float32)
            for tap_row in range(4):
                need_row = shift_row - tap_row + 1
                if need_row < -DR or need_row >= DR:
                    continue
                for tap_col in range(4):
                    need_col = shift_col - tap_col + 1
                    if need_col < -DL or need_col >= DL:
                        continue
                    hit = row_match[need_row] & col_match[need_col]
                    factor = factor + jnp.where(hit, tap_values[4 * tap_row + tap_col], 0.0)
            moved = jnp.roll(row_slab, -shift_col, axis=4)
            running = running + factor[:, None] * moved
    return running


def per_device(
    spectral, legendre, slot_pair, quad_weight, depart_code, stencil_pick, stencil_weight
):
    slot_local, row_local, col_total = spectral.shape
    height = depart_code.shape[2]
    slot_total = slot_pair.shape[0]
    wave_rank = lax.axis_index("wave")
    my_pairs = lax.dynamic_slice_in_dim(slot_pair, wave_rank * slot_local, slot_local)
    segment = lax.all_gather(spectral, "band", axis=1, tiled=True)
    row_count = segment.shape[1]
    masks = row_weights(my_pairs, jnp.arange(row_count, dtype=jnp.int32), M)
    masked = (segment.astype(jnp.float32)[:, :, None, None, :] * masks[..., None]).astype(
        jnp.bfloat16
    )
    leg_rows = legendre
    fourier = jnp.einsum(
        "sjohc,sij->isohc", masked, leg_rows, preferred_element_type=jnp.float32
    ).astype(jnp.bfloat16)
    by_latitude = lax.all_to_all(fourier, "wave", split_axis=0, concat_axis=1, tiled=True)
    left_rows = by_latitude.reshape(height, slot_total, 2, 2, LEV, FIELDS, 2)
    left_rows = left_rows.transpose(4, 5, 3, 0, 1, 2, 6).reshape(
        LEV * FIELDS * 2 * height, slot_total * 4
    )
    angle_rows = angle_table(slot_pair, M, NLON)
    grid_values = jnp.dot(left_rows, angle_rows, preferred_element_type=jnp.float32)
    grid_values = grid_values.astype(jnp.bfloat16).reshape(LEV, FIELDS, 2, height, NLON)
    extended = extended_2(grid_values, ((("band", "wave"), 3),), RIM)
    lat_rank = lax.axis_index(("band", "wave"))
    lat_devices = lax.axis_size(("band", "wave"))
    pole_rows = jnp.roll(jnp.flip(grid_values[:, :, :, :RIM], 3), NLON // 2, 4)
    equator_rows = jnp.flip(grid_values[:, :, ::-1, height - RIM :], 3)
    lower_rows = jnp.where(lat_rank == 0, pole_rows, extended[:, :, :, :RIM])
    upper_rows = jnp.where(
        lat_rank == lat_devices - 1, equator_rows, extended[:, :, :, height + RIM :]
    )
    padded = jnp.concatenate([lower_rows, grid_values, upper_rows], 3)
    selector = (jnp.arange(NSTEN, dtype=jnp.int32)[:, None] == stencil_pick.reshape(1, -1)).astype(
        jnp.float32
    )
    tap_table = jnp.dot(stencil_weight.T, selector, precision=lax.Precision.HIGHEST)

    def tap_weight(tap_index):
        return tap_table[tap_index].reshape(stencil_pick.shape)

    arrival = interpolate_window(padded, depart_code, tap_weight).astype(jnp.bfloat16)
    sums = lax.dot_general(
        arrival.reshape(-1, NLON),
        angle_rows,
        (((1,), (1,)), ((), ())),
        preferred_element_type=jnp.float32,
    )
    sums = sums.reshape(LEV, FIELDS, 2, height, slot_total, 2, 2)
    my_weight = lax.dynamic_slice_in_dim(quad_weight, wave_rank * height, height)
    scaling = my_weight[:, None, None] / (wave_factor(slot_pair, M)[None] * math.sqrt(NLON))
    coeffs = (sums * scaling[None, None, None, :, :, :, None]).astype(jnp.bfloat16)
    coeffs = coeffs.transpose(3, 4, 5, 2, 0, 1, 6).reshape(height, slot_total, 2, 2, col_total)
    by_wave = lax.all_to_all(coeffs, "wave", split_axis=1, concat_axis=0, tiled=True)
    leg_rows = legendre
    raw_sum = lax.psum_scatter(
        jnp.einsum("isohc,sij->jsohc", by_wave, leg_rows, preferred_element_type=jnp.float32)
        .reshape(row_local * lax.axis_size("band"), slot_local, 4 * col_total)
        .astype(jnp.bfloat16),
        "band",
        scatter_dimension=0,
        tiled=True,
    ).astype(jnp.float32)
    band_rank = lax.axis_index("band")
    masks = row_weights(my_pairs, band_rank * row_local + jnp.arange(row_local, dtype=jnp.int32), M)
    summed = jnp.einsum(
        "jsohc,sjoh->jsc",
        raw_sum.reshape(row_local, slot_local, 2, 2, col_total),
        masks,
        precision=lax.Precision.HIGHEST,
    )
    spectral_out = summed.transpose(1, 0, 2).astype(jnp.bfloat16)
    return (arrival, spectral_out)


def solution(mesh):
    in_specs = (
        P("wave", "band", None),
        P("wave", "band", None),
        P(),
        P("band"),
        P(None, None, ("band", "wave"), None),
        P(None, None, ("band", "wave"), None),
        P(),
    )
    out_specs = (P(None, None, None, ("band", "wave"), None), P("wave", "band", None))
    return jax.shard_map(
        per_device, mesh=mesh, in_specs=in_specs, out_specs=out_specs, check_vma=False
    )
```

profile of v0, /device:TPU:1, one launch (start us, length us, event | category | flops | bytes accessed | tf_op | source)
XLA Modules:
  0.0 900.5 jit_solution(3233454664386852259)
XLA Ops:
  11.1 26.1 %all_gather.3 = bf16[40,1408,8]{0,2,1:T(8,128)(2,1)S(1)} all-gather(bf16[40,88,8]{0,2,1:T(8,128)(2,1)S(1)} %copy.344), channel_id=1, replica_groups=mesh['band'=16,'wave'=16] {'band'}, dimensions={1}, use_global_device_ids=true | all-gather | bytes 957440 | tf_op jit(solution)/shard_map/all_gather | solution.py:105
  37.3 4.3 copy.345
  43.9 6.2 fusion.85
  52.9 13.7 %all-to-all-start = ((bf16[16,2,3200]{2,1,0:T(2,128)(2,1)}), bf16[16,2,3200]{2,1,0:T(2,128)(2,1)}, u32[]{:S(2)}, u32[]{:S(2)}) async-start(bf16[16,2,3200]{2,1,0:T(2,128)(2,1)} %reshape.2147), calls=%async_computation | async-start | bytes 409600 | tf_op jit(solution)/shard_map/all_to_all | solution.py:115
  69.0 12.2 %slice_reduce_fusion.15 = (f32[51200]{0:T(1024)S(1)}, f32[51200]{0:T(1024)}, f32[51200]{0:T(1024)}, f32[51200]{0:T(1024)}, f32[51200]{0:T(1024)S(1)}, /*index=5*...) fusion(f32[16,51200]{1,0:T(8,128)S(1)} %convolution_bitcast_fusion), kind=kLoop, calls=%fused_computation.236 | loop fusion | bytes 6553600 | tf_op jit(solution)/shard_map/slice | solution.py:139
  123.3 225.2 %fusion.188 = bf16[640,2,2,5120,1,1]{3,0,2,1,5,4:T(8,128)(2,1)} fusion(f32[640,2,2]{0,2,1:T(2,128)S(1)} %get-tuple-element.214, s32[640,2,2]{0,2,1:T(2,128)S(1)} %compare_select_fusion.7, f32[640,2,2]{0,2,1:T(2,128)S(1)} %get-tuple-element.213, pred[640,2,2]{0,2,1:T(4,128)(4,1)S(1)} %fusion.124), kind=kLoop, calls=%fused_computation.17.clone.clone.clone.clone.clone.clone.clone.clone.1 | loop fusion | flops 170393600 | bytes 26247680 | tf_op jit(solution)/shard_map/dot_general | solution.py:142
  352.5 9.8 %copy.348 = bf16[1,4,2,5,640,2,2]{3,2,1,6,5,4,0:T(2,128)(2,1)} copy(bf16[1,4,2,5,640,2,2]{4,6,1,2,5,3,0:T(2,128)(2,1)S(1)} %bitcast.188) | data formatting | bytes 409600 | tf_op jit(solution)/shard_map/transpose | solution.py:117
  362.3 14.7 %reshape.2052 = bf16[40,2560]{0,1:T(8,128)(2,1)S(1)} reshape(bf16[1,4,2,5,640,2,2]{3,2,1,6,5,4,0:T(2,128)(2,1)} %copy.348) | data formatting | bytes 409600 | tf_op jit(solution)/shard_map/reshape | solution.py:117
  377.0 226.8 %fusion.20 = bf16[40,5120]{1,0:T(8,128)(2,1)S(1)} fusion(bf16[40,2560]{0,1:T(8,128)(2,1)S(1)} %reshape.2052, f32[2560]{0:T(1024)S(1)} %compare_select_fusion.8, s32[2560]{0:T(1024)S(1)} %get-tuple-element.71, f32[2560]{0:T(1024)S(1)} %get-tuple-element.70, pred[2560]{0:T(1024)(128)(4,1)S(1)} %fusion.115), kind=kOutput, calls=%fused_computation.27 | convolution fusion | flops 1219174400 | bytes 647680 | tf_op jit(solution)/shard_map/dot_general | solution.py:121
  612.4 3.5 collective-permute-start
  615.9 18.4 %rev.6 = bf16[1,4,2,3,5120]{4,3,2,1,0:T(4,128)(2,1)} reverse(bf16[1,4,2,3,5120]{4,3,2,1,0:T(4,128)(2,1)} %get-tuple-element.203), dimensions={2,3} | reverse | bytes 491520 | tf_op jit(solution)/shard_map/jit(_flip)/rev | solution.py:127
  634.4 9.4 %slice.362 = bf16[1,4,2,3,2560]{4,3,2,1,0:T(4,128)(2,1)} reverse(bf16[1,4,2,3,2560]{4,3,2,1,0:T(4,128)(2,1)} %get-tuple-element.188), dimensions={3} | reverse | bytes 245760 | tf_op jit(solution)/shard_map/jit(_roll_static)/slice | solution.py:126
  643.7 6.3 slice.364
  657.4 3.1 fusion.138
  684.5 3.2 fusion.162
  688.4 35.6 %fusion.78 = bf16[1,4,2,5,5120]{4,3,2,1,0:T(8,128)(2,1)} fusion(f32[1,4,2,5,3]{4,3,2,1,0:T(8,128)} %get-tuple-element.243, f32[1,4,2,5,5117]{4,3,2,1,0:T(8,128)} %get-tuple-element.245, f32[1,4,2,5,2]{4,3,2,1,0:T(8,128)} %get-tuple-element.247, f32[1,4,2,5,5118]{4,3,2,1,0:T(8,128)} %get-tuple-element.249, f32[1,4,2,5,1]{4,3,2,1,0:T(8,128)} %get-tuple-element.251, ...), kind=kLoop, calls=%fused_computation.124 | loop fusion | flops 33792000 | bytes 45752320 | tf_op jit(solution)/shard_map/convert_element_type | solution.py:141
  724.0 13.2 %fusion.88 = bf16[5,640,2,2,1,4,2]{1,0,6,2,3,5,4:T(8,128)(2,1)S(1)} fusion(bf16[1,4,2,5,5120]{4,3,2,1,0:T(8,128)(2,1)} %fusion.78, f32[5,640,2]{1,0,2:T(8,128)} %broadcast_divide_fusion, bf16[640,2,2,5120,1,1]{3,0,2,1,5,4:T(8,128)(2,1)} %fusion.188), kind=kOutput, calls=%fused_computation.128 | convolution fusion | flops 1048780800 | bytes 26854400 | tf_op jit(solution)/shard_map/dot_general | solution.py:142
  737.3 4.4 copy.350
  741.8 3.7 reshape.2149
  745.5 17.4 %all_to_all.33 = bf16[16,2,3200]{2,1,0:T(2,128)(2,1)} all-to-all(bf16[16,2,3200]{2,1,0:T(2,128)(2,1)S(1)} %reshape.2149), channel_id=1, replica_groups=mesh['band'=16,'wave'=16] {'wave'}, dimensions={0} | all-to-all | bytes 409600 | tf_op jit(solution)/shard_map/all_to_all | solution.py:153
  762.9 10.4 %reshape.2150 = bf16[640,5,2,2,8]{4,3,2,1,0:T(2,128)(2,1)S(1)} reshape(bf16[16,2,3200]{2,1,0:T(2,128)(2,1)} %all_to_all.33) | data formatting | bytes 409600
  773.2 4.9 copy.366
  780.2 6.8 fusion.21
  790.3 100.9 %all-reduce.5.cloned.1.call-done = bf16[1408,40,32]{0,2,1:T(8,128)(2,1)} async-done(((bf16[1408,40,32]{0,2,1:T(8,128)(2,1)}), bf16[1408,40,32]{0,2,1:T(8,128)(2,1)}) %all-reduce.5.cloned.1.call-update) | async-done | bytes 3604496
  (207 shorter events, 104.5 us)
Async XLA Ops:
  7.2 60.2 %copy-start = (f32[16,16]{1,0:T(8,128)S(1)}, f32[16,16]{1,0:T(8,128)}, u32[]{:S(2)}) copy-start(f32[16,16]{1,0:T(8,128)} %param.13) | copy-start | bytes 3076
  50.1 17.1 %copy-start.40 = (s32[1,2,5,5120]{3,1,2,0:T(2,128)S(1)}, s32[1,2,5,5120]{3,1,2,0:T(2,128)}, u32[]{:S(2)}) copy-start(s32[1,2,5,5120]{3,1,2,0:T(2,128)} %param.12) | copy-start | bytes 614404
  52.9 296.4 %all-to-all-start = ((bf16[16,2,3200]{2,1,0:T(2,128)(2,1)}), bf16[16,2,3200]{2,1,0:T(2,128)(2,1)}, u32[]{:S(2)}, u32[]{:S(2)}) async-start(bf16[16,2,3200]{2,1,0:T(2,128)(2,1)} %reshape.2147), calls=%async_computation | async-start | bytes 409600 | tf_op jit(solution)/shard_map/all_to_all | solution.py:115
  66.7 824.5 %all-reduce.5.cloned.1.call-start = ((), (), s32[]{:S(2)}) async-start(), calls=%async_computation.2 | async-start | bytes 7208960
  88.8 7.7 copy-start.15
  90.0 2.8 copy-start.36
  91.2 3.0 copy-start.37
  91.2 5.3 copy-start.21
  91.2 6.6 copy-start.17
  92.8 3.7 copy-start.34
  92.8 5.0 copy-start.27
  94.2 3.7 copy-start.11
  94.2 3.7 copy-start.13
  97.9 2.9 copy-start.25
  105.8 2.6 copy-start.14
  105.8 2.6 copy-start.16
  105.9 2.6 copy-start.18
  105.9 2.6 copy-start.20
  123.3 225.3 %copy-start.45 = (f32[80]{0:T(128)S(1)}, f32[80]{0:T(128)}, u32[]{:S(2)}) copy-start(f32[80]{0:T(128)} %param.10) | copy-start | bytes 964
  609.8 40.3 %collective-permute-start.1 = (bf16[1,4,2,3,5120]{4,3,2,1,0:T(4,128)(2,1)}, bf16[1,4,2,3,5120]{4,3,2,1,0:T(4,128)(2,1)}, u32[]{:S(2)}, u32[]{:S(2)}) collective-permute-start(bf16[1,4,2,3,5120]{4,3,2,1,0:T(4,128)(2,1)} %get-tuple-element.202), channel_id=1, source_target_pairs={{1,0},{2,1},{3,2},{4,3},{5,4},{6,5},{7,6},{8,7},{9,8},{10,9},{11,1... | collective-permute-start | bytes 737288 | tf_op jit(solution)/shard_map/ppermute | solution.py:26
  612.4 38.8 %collective-permute-start = (bf16[1,4,2,3,5120]{4,3,2,1,0:T(4,128)(2,1)}, bf16[1,4,2,3,5120]{4,3,2,1,0:T(4,128)(2,1)}, u32[]{:S(2)}, u32[]{:S(2)}) collective-permute-start(bf16[1,4,2,3,5120]{4,3,2,1,0:T(4,128)(2,1)} %get-tuple-element.203), channel_id=1, source_target_pairs={{0,1},{1,2},{2,3},{3,4},{4,5},{5,6},{6,7},{7,8},{8,9},{9,10},{10,1... | collective-permute-start | bytes 737288 | tf_op jit(solution)/shard_map/ppermute | solution.py:25
  651.2 3.0 copy-start.30
  684.5 3.9 copy-start.41
  787.7 105.4 %copy-start.1 = (f32[16,16]{1,0:T(8,128)S(1)}, f32[16,16]{1,0:T(8,128)}, u32[]{:S(2)}) copy-start(f32[16,16]{1,0:T(8,128)} %param.13) | copy-start | bytes 3076
  (27 other events, 49.3 us)
Sparse Core Ops, SparseCore 0:
  787.1 104.0 all-reduce.4
where the time goes:
time: 909 us; the launch traced here: 900 us
  other arithmetic  302 us (33%)
  matrix products  254 us (28%)
  local copies, waits for them, and re-layouts  164 us (18%)
  waiting for transfers between devices  101 us (11%)
  blocking collectives  43.5 us (5%)
  starting transfers between devices  19.8 us (2%)
  between operations  16 us (2%)
    dot_general x1, matrix products, per_device(): jnp.dot(left_rows, angle_rows, preferred_element_type=jnp.float32)  227 us
    dot_general x1, other arithmetic, per_device(): lax.dot_general(arrival.reshape(-1, NLON), angle_rows, (((1,), (1,)), (()...  225 us
    unnamed x2, waiting for transfers between devices  101 us
    slice x24, local copies, waits for them, and re-layouts, interpolate_window(): moved = jnp.roll(row_slab, -shift_col, axis=4)  38.8 us
    convert_element_type x1, other arithmetic, per_device(): interpolate_window(padded, depart_code, tap_weight).astype(jnp.bfloat16)  35.6 us
    mul x18, other arithmetic, interpolate_window(): running = running + factor[:, None] * moved  30.5 us
    all_gather x1, blocking collectives, per_device(): segment = lax.all_gather(spectral, 'band', axis=1, tiled=True)  26.1 us
    unnamed x104, local copies, waits for them, and re-layouts  22.7 us
  transfers between devices with their start and end apart: 4, of which 1 were waited for; matrix products, arithmetic and copies ran while one was open for 35% of the time, Pallas kernels for 0%

commit v1 on v0

v1 whole, which is shorter than its diff:
```python
import functools
import math

import jax
import jax.numpy as jnp
import numpy as np
from jax import lax
from jax.experimental import pallas as pl
from jax.experimental.pallas import tpu as pltpu
from jax.sharding import PartitionSpec as P

M = 1280
NLON = 5120
FIELDS = 4
WAVES = 16
BANDS = 16
SLOTS = 40
ROWS = 88
NROW = ROWS * BANDS
LATS = 5
BAND_LATS = LATS * WAVES
Q1 = 40
Q2 = 128
M1 = 40
P2 = 16
SPAD = 48
LANES = 256
RIM = 3
MESH = pl.DeviceIdType.MESH
F32 = jnp.float32
BF16 = jnp.bfloat16
VMEM_LIMIT = 50 * 1024 * 1024
NT = (((1,), (1,)), ((), ()))
TN = (((0,), (0,)), ((), ()))


def phase_tables():
    m1 = np.arange(M1)[:, None, None]
    p2 = np.arange(P2)[None, :, None]
    q2 = np.arange(Q2)[None, None, :]
    e = np.zeros((M1, 2, 2, P2, 2, Q2))
    for o, m in enumerate((m1 + M1 * p2, m1 + M1 * (31 - p2))):
        a = 2 * np.pi * ((m * q2) % NLON) / NLON
        e[:, o, 0, :, 0] = np.cos(a)
        e[:, o, 0, :, 1] = np.sin(a)
        e[:, o, 1, :, 0] = -np.sin(a)
        e[:, o, 1, :, 1] = np.cos(a)
    a = 2 * np.pi * (np.outer(np.arange(Q1), np.arange(M1)) % M1) / M1
    t = np.zeros((Q1, 2, 2, 2, M1))
    for h in range(2):
        t[:, h, 0, h] = np.cos(a)
        t[:, h, 1, h] = -np.sin(a)
    t = t.reshape(Q1 * 2, 4 * M1)
    sel = np.zeros((LANES, 4, 128))
    for i in range(LATS):
        for o in range(2):
            for h in range(2):
                for f in range(FIELDS):
                    for r in range(2):
                        lane = i * 32 + ((o * 2 + h) * FIELDS + f) * 2 + r
                        sel[lane, o * 2 + r, (i * FIELDS + f) * 2 + h] = 1
    sel = sel.reshape(LANES, 512)
    return [
        v.astype(np.float32).astype(jnp.bfloat16)
        for v in (e.reshape(M1 * 64, 256), t, t.T.copy(), sel, sel.T.copy())
    ]


def exchange_kernel(axis, gather, src, dst, send_sem, recv_sem, own_sem):
    me = lax.axis_index(axis)
    count = 16
    barrier = pltpu.get_barrier_semaphore()
    for d in range(1, count):
        pl.semaphore_signal(
            barrier, inc=1, device_id={axis: lax.rem(me + d, count)}, device_id_type=MESH
        )
    pl.semaphore_wait(barrier, count - 1)
    copies = []
    for d in range(1, count):
        peer = lax.rem(me + d, count)
        copy = pltpu.make_async_remote_copy(
            src_ref=src if gather else src.at[peer],
            dst_ref=dst.at[me],
            send_sem=send_sem.at[d],
            recv_sem=recv_sem.at[d],
            device_id={axis: peer},
            device_id_type=MESH,
        )
        copy.start()
        copies.append(copy)
    own = pltpu.make_async_copy(src if gather else src.at[me], dst.at[me], own_sem)
    own.start()
    own.wait()
    for copy in copies:
        copy.wait()


def exchange(x, axis, gather, cid):
    shape = ((16,) + x.shape) if gather else x.shape
    return pl.pallas_call(
        functools.partial(exchange_kernel, axis, gather),
        out_shape=jax.ShapeDtypeStruct(shape, x.dtype),
        in_specs=[pl.BlockSpec(memory_space=pl.ANY)],
        out_specs=pl.BlockSpec(memory_space=pl.ANY),
        scratch_shapes=[
            pltpu.SemaphoreType.DMA((16,)),
            pltpu.SemaphoreType.DMA((16,)),
            pltpu.SemaphoreType.DMA,
        ],
        compiler_params=pltpu.CompilerParams(collective_id=cid, has_side_effects=True),
    )(x)


def halo_kernel(grid, before, after, send_sem, recv_sem):
    band, wave = lax.axis_index("band"), lax.axis_index("wave")
    rank = band * WAVES + wave
    total = BANDS * WAVES
    nxt, prv = lax.rem(rank + 1, total), lax.rem(rank + total - 1, total)
    ids = [{"band": r // WAVES, "wave": lax.rem(r, WAVES)} for r in (nxt, prv)]
    barrier = pltpu.get_barrier_semaphore()
    for where in ids:
        pl.semaphore_signal(barrier, inc=1, device_id=where, device_id_type=MESH)
    pl.semaphore_wait(barrier, 2)
    copies = []
    for k, (src, dst) in enumerate(((grid.at[pl.ds(2, RIM)], before), (grid.at[pl.ds(0, RIM)], after))):
        copy = pltpu.make_async_remote_copy(
            src_ref=src,
            dst_ref=dst,
            send_sem=send_sem.at[k],
            recv_sem=recv_sem.at[k],
            device_id=ids[k],
            device_id_type=MESH,
        )
        copy.start()
        copies.append(copy)
    for copy in copies:
        copy.wait()


def halo(grid, cid):
    shape = jax.ShapeDtypeStruct((RIM,) + grid.shape[1:], grid.dtype)
    return pl.pallas_call(
        halo_kernel,
        out_shape=(shape, shape),
        in_specs=[pl.BlockSpec(memory_space=pl.ANY)],
        out_specs=(pl.BlockSpec(memory_space=pl.ANY),) * 2,
        scratch_shapes=[pltpu.SemaphoreType.DMA((2,)), pltpu.SemaphoreType.DMA((2,))],
        compiler_params=pltpu.CompilerParams(collective_id=cid, has_side_effects=True),
    )(grid)


GROUP = 4


def row_marks(pair, shape):
    j = lax.broadcasted_iota(jnp.int32, shape, 1)
    low_count = M - pair
    higher = j >= low_count
    degree = jnp.where(higher, j - low_count, j)
    sign = (1 - 2 * (degree & 1)).astype(F32)
    return higher, jnp.where(j <= M, 1.0, 0.0), sign


def to_latitude_kernel(pairs, spec, leg, out, rows, held):
    g = pl.program_id(0)
    for b in range(BANDS):
        rows[:, ROWS * b : ROWS * (b + 1)] = spec[b].astype(F32)[:, :ROWS]
    for k in range(GROUP):
        s = g * GROUP + k
        pair = pairs[s]
        value = rows[8 * k : 8 * k + 8, :]
        higher, used, sign = row_marks(pair, (8, NROW))
        value = value * used
        low = jnp.where(higher, 0.0, value) * jnp.where(pair == 0, 1.0, 2.0)
        high = jnp.where(higher, value, 0.0) * 2.0
        x = jnp.concatenate([low, low * sign, high, high * sign], axis=0).astype(BF16)
        held[pl.ds(BAND_LATS * s, BAND_LATS), 0:32] = lax.dot_general(
            leg[k], x, NT, preferred_element_type=F32
        )

    @pl.when(g == SLOTS // GROUP - 1)
    def _():
        for w in range(WAVES):
            part = [held[pl.ds(LATS * w + i, SLOTS, stride=BAND_LATS), :][:, 0:32] for i in range(LATS)]
            first = jnp.concatenate(part[:4], axis=1)
            second = jnp.concatenate([part[4], jnp.zeros((SLOTS, 96), F32)], axis=1)
            both = jnp.concatenate([first, second], axis=1)
            both = jnp.concatenate([both, jnp.zeros((SPAD - SLOTS, LANES), F32)], axis=0)
            out[w] = both.astype(BF16)


def to_latitude(pairs, spec, leg):
    return pl.pallas_call(
        to_latitude_kernel,
        grid=(SLOTS // GROUP,),
        out_shape=jax.ShapeDtypeStruct((WAVES, SPAD, LANES), BF16),
        in_specs=[
            pl.BlockSpec(memory_space=pltpu.SMEM),
            pl.BlockSpec((BANDS, 8 * GROUP, 128), lambda g: (0, g, 0)),
            pl.BlockSpec((GROUP, BAND_LATS, NROW), lambda g: (g, 0, 0)),
        ],
        out_specs=pl.BlockSpec((WAVES, SPAD, LANES), lambda g: (0, 0, 0)),
        scratch_shapes=[pltpu.VMEM((8 * GROUP, NROW), F32), pltpu.VMEM((SLOTS * BAND_LATS, 128), F32)],
        compiler_params=pltpu.CompilerParams(vmem_limit_bytes=VMEM_LIMIT),
    )(pairs, spec, leg)


def to_degree_kernel(pairs, coef, leg, out, held):
    g = pl.program_id(0)

    @pl.when(g == 0)
    def _():
        for w in range(WAVES):
            block = coef[w].astype(F32)
            for i in range(LATS):
                held[pl.ds(LATS * w + i, SLOTS, stride=BAND_LATS), :] = jnp.concatenate(
                    [block[:SLOTS, 32 * i : 32 * i + 32], jnp.zeros((SLOTS, 96), F32)], axis=1
                )

    for k in range(GROUP):
        s = g * GROUP + k
        mine = held[pl.ds(BAND_LATS * s, BAND_LATS), :][:, 0:32].astype(BF16)
        both = lax.dot_general(mine, leg[k], TN, preferred_element_type=F32)
        higher, used, sign = row_marks(pairs[s], (8, NROW))
        low = both[0:8] + sign * both[8:16]
        high = both[16:24] + sign * both[24:32]
        total = jnp.where(higher, high, low) * used
        for b in range(BANDS):
            out[b, 8 * k : 8 * k + 8, :] = jnp.concatenate(
                [total[:, ROWS * b : ROWS * (b + 1)], jnp.zeros((8, 128 - ROWS), F32)], axis=1
            ).astype(BF16)


def to_degree(pairs, coef, leg):
    return pl.pallas_call(
        to_degree_kernel,
        grid=(SLOTS // GROUP,),
        out_shape=jax.ShapeDtypeStruct((BANDS, 8 * SLOTS, 128), BF16),
        in_specs=[
            pl.BlockSpec(memory_space=pltpu.SMEM),
            pl.BlockSpec((WAVES, SPAD, LANES), lambda g: (0, 0, 0)),
            pl.BlockSpec((GROUP, BAND_LATS, NROW), lambda g: (g, 0, 0)),
        ],
        out_specs=pl.BlockSpec((BANDS, 8 * GROUP, 128), lambda g: (0, g, 0)),
        scratch_shapes=[pltpu.VMEM((SLOTS * BAND_LATS, 128), F32)],
        compiler_params=pltpu.CompilerParams(vmem_limit_bytes=VMEM_LIMIT),
    )(pairs, coef, leg)


def to_grid_kernel(place, four, phase, dft, sel, grid, by_pair, mixed):
    row = lax.broadcasted_iota(jnp.int32, (640, WAVES * SPAD), 0)
    onehot = jnp.where(row == place[...], 1.0, 0.0).astype(BF16)
    ordered = jnp.dot(onehot, four[...], preferred_element_type=F32).astype(BF16)
    by_pair[...] = jnp.dot(ordered, sel[...], preferred_element_type=F32).astype(BF16)
    for m1 in range(M1):
        low, high = pl.ds(P2 * m1, P2), pl.ds(P2 * (M1 - 1 - m1), P2)
        left = jnp.concatenate(
            [by_pair[low, 0:128], by_pair[low, 128:256], by_pair[high, 256:384], by_pair[high, 384:512]],
            axis=0,
        )
        part = lax.dot_general(left, phase[64 * m1 : 64 * m1 + 64, :], TN, preferred_element_type=F32)
        mixed[pl.ds(m1, 40, stride=M1), :] = part[0:40, 0:128]
        mixed[pl.ds(1600 + m1, 40, stride=M1), :] = part[0:40, 128:256]
    for n in range(LATS * FIELDS):
        right = jnp.concatenate(
            [mixed[80 * n : 80 * n + 80, :], mixed[1600 + 80 * n : 1680 + 80 * n, :]], axis=0
        ).astype(BF16)
        grid[n // FIELDS, n % FIELDS] = jnp.dot(dft[...], right, preferred_element_type=F32).astype(BF16)


def whole(n):
    return [pl.BlockSpec(memory_space=pltpu.VMEM)] * n


def to_grid(place, four, phase, dft, sel):
    return pl.pallas_call(
        to_grid_kernel,
        out_shape=jax.ShapeDtypeStruct((LATS, FIELDS, 80, Q2), BF16),
        in_specs=whole(5),
        out_specs=whole(1)[0],
        scratch_shapes=[pltpu.VMEM((640, 512), BF16), pltpu.VMEM((3200, 128), F32)],
        compiler_params=pltpu.CompilerParams(vmem_limit_bytes=VMEM_LIMIT),
    )(place, four, phase, dft, sel)


def shifted(x, by, lane):
    if by == 0:
        return x
    if by > 0:
        carried = jnp.concatenate([x[2:], x[:2]], axis=0)
        return pltpu.roll(jnp.where(lane < by, carried, x), Q2 - by, 1)
    carried = jnp.concatenate([x[78:], x[:78]], axis=0)
    return pltpu.roll(jnp.where(lane >= Q2 + by, carried, x), -by, 1)


def spread(values, bit, step):
    n = len(values)
    out = []
    for k in range(n + step):
        keep = values[k] if k < n else 0.0
        moved = values[k - step] if k >= step else 0.0
        out.append(jnp.where(bit, moved, keep))
    return out


def stencil_kernel(
    rank, grid, before, after, code, pick, weight, quad, place, phase, dft_back, sel_back,
    arrival, back, ext, moved, summed, mixed, by_pair,
):
    lane = lax.broadcasted_iota(jnp.int32, (80, Q2), 1)
    row_odd = (lax.broadcasted_iota(jnp.int32, (80, Q2), 0) & 1) == 1
    for f in range(FIELDS):
        for i in range(LATS):
            ext[RIM + i, f] = grid[i, f].astype(F32)
        for k in range(RIM):
            ext[k, f] = before[k, f].astype(F32)
            ext[RIM + LATS + k, f] = after[k, f].astype(F32)

    @pl.when(rank[0] == 0)
    def _():
        for f in range(FIELDS):
            for k in range(RIM):
                x = grid[RIM - 1 - k, f].astype(F32)
                ext[k, f] = jnp.concatenate([x[40:], x[:40]], axis=0)

    @pl.when(rank[0] == BANDS * WAVES - 1)
    def _():
        for f in range(FIELDS):
            for k in range(RIM):
                x = grid[LATS - 1 - k, f].astype(F32)
                up = jnp.concatenate([x[1:], x[:1]], axis=0)
                down = jnp.concatenate([x[79:], x[:79]], axis=0)
                ext[RIM + LATS + k, f] = jnp.where(row_odd, down, up)

    def shift_row(n, _):
        x = ext[n // FIELDS, lax.rem(n, FIELDS)]
        for c in range(7):
            moved[c, n // FIELDS, lax.rem(n, FIELDS)] = shifted(x, c - 3, lane)
        return 0

    lax.fori_loop(0, (LATS + 2 * RIM) * FIELDS, shift_row, 0)

    def chunk(n, _):
        i, start = n // 10, pl.multiple_of(lax.rem(n, 10) * 8, 8)
        at = pl.multiple_of(n * 8, 8)
        e = code[pl.ds(at, 8), :]
        t = pick[pl.ds(at, 8), :]
        taps = [
            jnp.take_along_axis(jnp.broadcast_to(weight[k : k + 1, :], (8, 128)), t, axis=1)
            for k in range(16)
        ]
        x0, x1 = (e & 1) == 1, (e & 2) == 2
        y0, y1 = (e & 4) == 4, (e & 8) == 8
        columns = [spread([taps[4 * a + b] for a in range(4)], y0, 1) for b in range(4)]
        columns = [spread(column, y1, 2) for column in columns]
        total = [jnp.zeros((8, 128), F32) for _ in range(FIELDS)]
        for sr in range(7):
            factors = spread(spread([columns[b][sr] for b in range(4)], x0, 1), x1, 2)
            for sc in range(7):
                for f in range(FIELDS):
                    total[f] = total[f] + factors[sc] * moved[sc, i + sr, f, pl.ds(start, 8), :]
        for f in range(FIELDS):
            summed[i, f, pl.ds(start, 8), :] = total[f]
        return 0

    lax.fori_loop(0, 50, chunk, 0)
    for n in range(LATS * FIELDS):
        i, f = n // FIELDS, n % FIELDS
        value = summed[i, f].astype(BF16)
        arrival[f, 80 * i : 80 * i + 80, :] = value
        both = jnp.dot(dft_back[...], value, preferred_element_type=F32)
        mixed[80 * n : 80 * n + 80, :] = both[0:80]
        mixed[1600 + 80 * n : 1680 + 80 * n, :] = both[80:160]
    by_pair[...] = jnp.zeros((640, 512), BF16)
    for m1 in range(M1):
        right = jnp.concatenate(
            [mixed[pl.ds(m1, 40, stride=M1), :], mixed[pl.ds(1600 + m1, 40, stride=M1), :]], axis=1
        ).astype(BF16)
        part = lax.dot_general(phase[64 * m1 : 64 * m1 + 64, :], right, NT, preferred_element_type=F32)
        part = (part * quad[:, 0:40]).astype(BF16)
        low, high = pl.ds(P2 * m1, P2), pl.ds(P2 * (M1 - 1 - m1), P2)
        for k, where in enumerate((low, low, high, high)):
            by_pair[where, 128 * k : 128 * k + 40] = part[16 * k : 16 * k + 16]
    ordered = jnp.dot(by_pair[...], sel_back[...], preferred_element_type=F32).astype(BF16)
    column = lax.broadcasted_iota(jnp.int32, (WAVES * SPAD, 640), 1)
    onehot = jnp.where(column == place[...], 1.0, 0.0).astype(BF16)
    back[...] = jnp.dot(onehot, ordered, preferred_element_type=F32).astype(BF16)


def stencil(rank, grid, before, after, code, pick, weight, quad, place, phase, dft_back, sel_back):
    return pl.pallas_call(
        stencil_kernel,
        out_shape=(
            jax.ShapeDtypeStruct((FIELDS, 2 * LATS * Q1, Q2), BF16),
            jax.ShapeDtypeStruct((WAVES * SPAD, LANES), BF16),
        ),
        in_specs=[pl.BlockSpec(memory_space=pltpu.SMEM)] + whole(11),
        out_specs=tuple(whole(2)),
        scratch_shapes=[
            pltpu.VMEM((LATS + 2 * RIM, FIELDS, 80, Q2), F32),
            pltpu.VMEM((7, LATS + 2 * RIM, FIELDS, 80, Q2), F32),
            pltpu.VMEM((LATS, FIELDS, 80, Q2), F32),
            pltpu.VMEM((3200, 128), F32),
            pltpu.VMEM((640, 512), BF16),
        ],
        compiler_params=pltpu.CompilerParams(vmem_limit_bytes=VMEM_LIMIT),
    )(rank, grid, before, after, code, pick, weight, quad, place, phase, dft_back, sel_back)


def grid_view(x):
    return x.reshape(2, LATS, Q1, Q2).transpose(1, 2, 0, 3).reshape(2 * LATS * Q1, Q2)


def per_device(
    spectral, legendre, slot_pair, quad_weight, depart_code, stencil_pick, stencil_weight
):
    phase, dft, dft_back, sel, sel_back = [jnp.asarray(t) for t in phase_tables()]
    wave_rank = lax.axis_index("wave")
    band_rank = lax.axis_index("band")
    pairs = lax.dynamic_slice_in_dim(slot_pair, wave_rank * SLOTS, SLOTS)
    place = (slot_pair % M1) * P2 + slot_pair // M1
    place = jnp.pad(place.reshape(WAVES, SLOTS), ((0, 0), (0, SPAD - SLOTS)), constant_values=-1)
    rank = (band_rank * WAVES + wave_rank).reshape(1)
    my_weight = lax.dynamic_slice_in_dim(quad_weight, wave_rank * LATS, LATS)
    quad = jnp.repeat(my_weight / math.sqrt(NLON), 2 * FIELDS)
    quad = jnp.pad(quad, (0, 128 - quad.shape[0])).reshape(1, 128)
    weight = jnp.pad(stencil_weight.T, ((0, 0), (0, 112)))

    own = spectral.transpose(0, 2, 1).reshape(8 * SLOTS, ROWS)
    own = jnp.pad(own, ((0, 0), (0, 128 - ROWS)))
    spec = exchange(own, "band", True, 1)
    four = to_latitude(pairs, spec, legendre)
    four = exchange(four, "wave", False, 2)
    grid = to_grid(place.reshape(1, -1), four.reshape(WAVES * SPAD, LANES), phase, dft, sel)
    before, after = halo(grid, 3)
    arrival, back = stencil(
        rank, grid, before, after, grid_view(depart_code), grid_view(stencil_pick), weight, quad,
        place.reshape(-1, 1), phase, dft_back, sel_back,
    )
    back = exchange(back.reshape(WAVES, SPAD, LANES), "wave", False, 4)
    parts = to_degree(pairs, back, legendre)
    parts = exchange(parts, "band", False, 5)
    total = jnp.sum(parts.astype(F32), axis=0).astype(BF16)
    spectral_out = total.reshape(SLOTS, 8, 128)[:, :, :ROWS].transpose(0, 2, 1)
    arrival = arrival.reshape(FIELDS, LATS, Q1, 2, Q2).transpose(0, 3, 1, 2, 4)
    return arrival.reshape(1, FIELDS, 2, LATS, NLON), spectral_out


def solution(mesh):
    lat = ("band", "wave")
    in_specs = (
        P("wave", "band", None),
        P("wave", "band", None),
        P(),
        P("band"),
        P(None, None, lat, None),
        P(None, None, lat, None),
        P(),
    )
    out_specs = (P(None, None, None, lat, None), P("wave", "band", None))
    return jax.shard_map(
        per_device, mesh=mesh, in_specs=in_specs, out_specs=out_specs, check_vma=False
    )
```

time: 909 us -> 147 us (0.16)
  other arithmetic: 302 us -> 2.93 us
  matrix products: 254 us -> 0 us
  local copies, waits for them, and re-layouts: 164 us -> 13.7 us
  Pallas kernels: 0 us -> 127 us
  waiting for transfers between devices: 101 us -> 0 us
  blocking collectives: 43.5 us -> 0 us
  starting transfers between devices: 19.8 us -> 0 us
  between operations: 16 us -> 0.86 us
    dot_general x5 -> x0, matrix products: 254 us -> none  [the longest x1 227 us: per_device(): jnp.dot(left_rows, angle_rows, preferred_element_type=jnp.float32)]
    dot_general x2 -> x0, other arithmetic: 226 us -> none  [the longest x1 225 us: per_device(): lax.dot_general(arrival.reshape(-1, NLON), angle_rows, (((1,), (1,)), (()...]
    pallas_call x0 -> x9, Pallas kernels: none -> 127 us  [the longest x4 82.9 us: exchange(): pl.pallas_call(functools.partial(exchange_kernel, axis, gather), out_shap...]
    unnamed x2 -> x0, waiting for transfers between devices: 101 us -> none
    slice x29 -> x0, local copies, waits for them, and re-layouts: 68.4 us -> none  [the longest x24 38.8 us: interpolate_window(): moved = jnp.roll(row_slab, -shift_col, axis=4)]
    convert_element_type x7 -> x0, other arithmetic: 38.8 us -> none  [the longest x1 35.6 us: per_device(): interpolate_window(padded, depart_code, tap_weight).astype(jnp.bfloat16)]
    mul x22 -> x0, other arithmetic: 31.3 us -> none  [the longest x18 30.5 us: interpolate_window(): running = running + factor[:, None] * moved]
    all_gather x1 -> x0, blocking collectives: 26.1 us -> none  [per_device(): segment = lax.all_gather(spectral, 'band', axis=1, tiled=True)]
  transfers between devices with their start and end apart: 4 -> 0, of which waited for: 1 -> 0; matrix products, arithmetic and copies ran while one was open for 35% -> 0% of each run, Pallas kernels for 0% -> 0%
where the time goes in v1:
time: 147 us; the launch traced here: 145 us
  Pallas kernels  127 us (86%)
  local copies, waits for them, and re-layouts  13.7 us (9%)
  other arithmetic  2.93 us (2%)
    pallas_call x4, Pallas kernels, exchange(): pl.pallas_call(functools.partial(exchange_kernel, axis, gather), out_shap...  82.9 us
    pallas_call x1, Pallas kernels, stencil(): pl.pallas_call(stencil_kernel, out_shape=(jax.ShapeDtypeStruct((FIELDS, 2...  15.1 us
    unnamed x35, local copies, waits for them, and re-layouts  10.3 us
    pallas_call x1, Pallas kernels, to_latitude(): pl.pallas_call(to_latitude_kernel, grid=(SLOTS // GROUP,), out_shape=jax....  9.87 us
    pallas_call x1, Pallas kernels, to_degree(): pl.pallas_call(to_degree_kernel, grid=(SLOTS // GROUP,), out_shape=jax.Sh...  9.21 us
    pallas_call x1, Pallas kernels, halo(): pl.pallas_call(halo_kernel, out_shape=(shape, shape), in_specs=[pl.BlockS...  7.71 us

profile of v1, /device:TPU:1, one launch (start us, length us, event | category | flops | bytes accessed | tf_op | source)
XLA Modules:
  0.0 144.6 jit_solution(11993068447488783905)
XLA Ops:
  0.6 0.8 dynamic_slice.6.pairs
  1.4 0.7 dynamic-slice_multiply_fusion
  3.2 0.8 copy.20
  4.0 1.5 %pad.17.src = bf16[320,128]{1,0:T(8,128)(2,1)} pad(bf16[320,88]{1,0:T(8,128)(2,1)} %bitcast.32, bf16[]{:T(256)} %constant.52.clone.1), padding=0_0x0_40 | pad | bytes 138242 | tf_op jit(solution)/shard_map/jit(_pad)/pad | solution.py:430
  5.7 23.2 %shard_map.131.spec = bf16[16,320,128]{2,1,0:T(8,128)(2,1)} custom-call(bf16[320,128]{1,0:T(8,128)(2,1)} %pad.17.src), custom_call_target="tpu_custom_call" | custom-call | tf_op jit(solution)/shard_map/pallas_call | solution.py:100
  28.9 1.3 copy-done.2
  30.2 9.9 %shard_map.132.src = bf16[16,48,256]{2,1,0:T(8,128)(2,1)S(1)} custom-call(s32[40]{0:T(128)S(1)} %dynamic_slice.6.pairs, bf16[16,320,128]{2,1,0:T(8,128)(2,1)S(1)} %copy-done.2, bf16[40,80,1408]{2,1,0:T(8,128)(2,1)} %leg.3), custom_call_target="tpu_custom_call" | custom-call | tf_op jit(solution)/shard_map/pallas_call | solution.py:193
  40.1 0.7 copy-done.6
  40.9 19.6 %shard_map.133 = bf16[16,48,256]{2,1,0:T(8,128)(2,1)} custom-call(bf16[16,48,256]{2,1,0:T(8,128)(2,1)} %copy-done.6), custom_call_target="tpu_custom_call" | custom-call | tf_op jit(solution)/shard_map/pallas_call | solution.py:100
  60.5 1.0 copy-done.7
  61.5 2.3 %shard_map.134.grid = bf16[5,4,80,128]{3,2,1,0:T(8,128)(2,1)S(1)} custom-call(s32[1,768]{1,0:T(1,128)S(1)} %reshape.54.place, bf16[768,256]{1,0:T(8,128)(2,1)S(1)} %bitcast.27, bf16[2560,256]{1,0:T(8,128)(2,1)S(1)} %copy-done, bf16[80,160]{1,0:T(8,128)(2,1)S(1)} %copy-done.16, bf16[256,512]{1,0:T(8,128)(2,1)S(1)} %copy-done.10), custom_call_target="tpu_custom_call" | custom-call | tf_op jit(solution)/shard_map/pallas_call | solution.py:276
  63.8 0.7 copy-done.3
  64.6 7.7 %shard_map.135 = (bf16[3,4,80,128]{3,2,1,0:T(8,128)(2,1)}, bf16[3,4,80,128]{3,2,1,0:T(8,128)(2,1)}) custom-call(bf16[5,4,80,128]{3,2,1,0:T(8,128)(2,1)} %copy-done.3), custom_call_target="tpu_custom_call" | custom-call | tf_op jit(solution)/shard_map/pallas_call | solution.py:142
  72.3 1.0 copy-done.4
  73.3 0.9 copy-done.11
  74.3 0.9 copy-done.12
  75.2 15.1 %shard_map.136 = (bf16[4,400,128]{2,1,0:T(8,128)(2,1)}, bf16[768,256]{1,0:T(8,128)(2,1)S(1)}) custom-call(s32[1]{0:T(128)} %bitcast.rank, bf16[5,4,80,128]{3,2,1,0:T(8,128)(2,1)S(1)} %copy-done.4, bf16[3,4,80,128]{3,2,1,0:T(8,128)(2,1)S(1)} %copy-done.11, bf16[3,4,80,128]{3,2,1,0:T(8,128)(2,1)S(1)} %copy-done.12, s32[400,128]{1,0:T(8,128)S(1)} %bitcast.29, ...), custom_call_target="tpu_custom_call" | custom-call | tf_op jit(solution)/shard_map/pallas_call | solution.py:391
  90.4 0.7 copy-done.8
  91.1 18.3 %shard_map.137.coef = bf16[16,48,256]{2,1,0:T(8,128)(2,1)} custom-call(bf16[16,48,256]{2,1,0:T(8,128)(2,1)} %bitcast.28), custom_call_target="tpu_custom_call" | custom-call | tf_op jit(solution)/shard_map/pallas_call | solution.py:100
  109.4 1.0 copy-done.5
  110.4 9.2 %shard_map.138.src = bf16[16,320,128]{2,1,0:T(8,128)(2,1)S(1)} custom-call(s32[40]{0:T(128)S(1)} %dynamic_slice.6.pairs, bf16[16,48,256]{2,1,0:T(8,128)(2,1)S(1)} %copy-done.5, bf16[40,80,1408]{2,1,0:T(8,128)(2,1)} %leg.3), custom_call_target="tpu_custom_call" | custom-call | tf_op jit(solution)/shard_map/pallas_call | solution.py:235
  119.6 1.1 copy-done.1
  120.7 21.7 %shard_map.139 = bf16[16,320,128]{2,1,0:T(8,128)(2,1)} custom-call(bf16[16,320,128]{2,1,0:T(8,128)(2,1)} %copy-done.1), custom_call_target="tpu_custom_call" | custom-call | tf_op jit(solution)/shard_map/pallas_call | solution.py:100
  142.5 1.5 %reduce_sum.12 = bf16[320,128]{1,0:T(8,128)(2,1)S(1)} reduce(bf16[16,320,128]{2,1,0:T(8,128)(2,1)} %shard_map.139, bf16[]{:T(256)} %constant.52.clone.1), dimensions={0}, to_apply=%region_0.1 | reduce | flops 614400 | bytes 1392642 | tf_op jit(solution)/shard_map/reduce_sum | solution.py:443
  (34 shorter events, 1.9 us)
Async XLA Ops:
  28.9 1.3 copy-start.2
  30.2 30.2 %copy-start = (bf16[2560,256]{1,0:T(8,128)(2,1)S(1)}, bf16[2560,256]{1,0:T(8,128)(2,1)}, u32[]{:S(2)}) copy-start(bf16[2560,256]{1,0:T(8,128)(2,1)} %constant.57.clone.phase) | copy-start | bytes 3932164
  30.2 30.2 %copy-start.10 = (bf16[256,512]{1,0:T(8,128)(2,1)S(1)}, bf16[256,512]{1,0:T(8,128)(2,1)}, u32[]{:S(2)}) copy-start(bf16[256,512]{1,0:T(8,128)(2,1)} %constant.60.clone.sel) | copy-start | bytes 786436
  30.2 30.3 %copy-start.16 = (bf16[80,160]{1,0:T(8,128)(2,1)S(1)}, bf16[80,160]{1,0:T(8,128)(2,1)}, u32[]{:S(2)}) copy-start(bf16[80,160]{1,0:T(8,128)(2,1)} %constant.58.clone.dft) | copy-start | bytes 76804
  40.1 0.7 copy-start.6
  60.5 1.0 copy-start.7
  61.5 10.8 %copy-start.9 = (bf16[512,256]{1,0:T(8,128)(2,1)S(1)}, bf16[512,256]{1,0:T(8,128)(2,1)}, u32[]{:S(2)}) copy-start(bf16[512,256]{1,0:T(8,128)(2,1)} %constant.61.clone.sel_back) | copy-start | bytes 786436
  61.5 10.8 %copy-start.13 = (s32[1,2,5,5120]{3,1,2,0:T(2,128)S(1)}, s32[1,2,5,5120]{3,1,2,0:T(2,128)}, u32[]{:S(2)}) copy-start(s32[1,2,5,5120]{3,1,2,0:T(2,128)} %param.16) | copy-start | bytes 614404
  61.5 10.8 %copy-start.14 = (s32[1,2,5,5120]{3,1,2,0:T(2,128)S(1)}, s32[1,2,5,5120]{3,1,2,0:T(2,128)}, u32[]{:S(2)}) copy-start(s32[1,2,5,5120]{3,1,2,0:T(2,128)} %param.17) | copy-start | bytes 614404
  61.5 10.8 %copy-start.15 = (bf16[160,80]{1,0:T(8,128)(2,1)S(1)}, bf16[160,80]{1,0:T(8,128)(2,1)}, u32[]{:S(2)}) copy-start(bf16[160,80]{1,0:T(8,128)(2,1)} %constant.59.clone.dft_back) | copy-start | bytes 76804
  63.8 0.8 copy-start.3
  72.3 1.0 copy-start.4
  73.3 0.9 copy-start.11
  74.3 0.9 copy-start.12
  90.4 0.8 copy-start.8
  109.4 1.0 copy-start.5
  119.6 1.1 copy-start.1

commit v2 on v1

v2 whole, which is shorter than its diff:
```python
import functools
import math

import jax
import jax.numpy as jnp
import numpy as np
from jax import lax
from jax.experimental import pallas as pl
from jax.experimental.pallas import tpu as pltpu
from jax.sharding import PartitionSpec as P

M = 1280
NLON = 5120
FIELDS = 4
WAVES = 16
BANDS = 16
SLOTS = 40
ROWS = 88
NROW = ROWS * BANDS
LATS = 5
BAND_LATS = LATS * WAVES
Q1 = 40
Q2 = 128
M1 = 40
P2 = 16
LANES = 256
RIM = 3
MESH = pl.DeviceIdType.MESH
F32 = jnp.float32
BF16 = jnp.bfloat16
VMEM_LIMIT = 50 * 1024 * 1024
NT = (((1,), (1,)), ((), ()))
TN = (((0,), (0,)), ((), ()))


def phase_tables():
    m1 = np.arange(M1)[:, None, None]
    p2 = np.arange(P2)[None, :, None]
    q2 = np.arange(Q2)[None, None, :]
    e = np.zeros((M1, 2, 2, P2, 2, Q2))
    for o, m in enumerate((m1 + M1 * p2, m1 + M1 * (31 - p2))):
        a = 2 * np.pi * ((m * q2) % NLON) / NLON
        e[:, o, 0, :, 0] = np.cos(a)
        e[:, o, 0, :, 1] = np.sin(a)
        e[:, o, 1, :, 0] = -np.sin(a)
        e[:, o, 1, :, 1] = np.cos(a)
    a = 2 * np.pi * (np.outer(np.arange(Q1), np.arange(M1)) % M1) / M1
    t = np.zeros((Q1, 2, 2, 2, M1))
    for h in range(2):
        t[:, h, 0, h] = np.cos(a)
        t[:, h, 1, h] = -np.sin(a)
    t = t.reshape(Q1 * 2, 4 * M1)
    sel = np.zeros((LANES, 4, 128))
    for i in range(LATS):
        for o in range(2):
            for h in range(2):
                for f in range(FIELDS):
                    for r in range(2):
                        lane = i * 32 + ((o * 2 + h) * FIELDS + f) * 2 + r
                        sel[lane, o * 2 + r, (i * FIELDS + f) * 2 + h] = 1
    sel = sel.reshape(LANES, 512)
    return [
        v.astype(np.float32).astype(jnp.bfloat16)
        for v in (e.reshape(M1 * 64, 256), t, t.T.copy(), sel, sel.T.copy())
    ]


GROUPS = 5
GROUP = SLOTS // GROUPS
TALL = 8 * GROUP
SIDE = 4


def row_marks(pair, shape):
    j = lax.broadcasted_iota(jnp.int32, shape, 1)
    low_count = M - pair
    higher = j >= low_count
    degree = jnp.where(higher, j - low_count, j)
    sign = (1 - 2 * (degree & 1)).astype(F32)
    return higher, jnp.where(j <= M, 1.0, 0.0), sign


class Plane:
    def __init__(self, g):
        band = lax.axis_index("band")
        x, y = band // SIDE, lax.rem(band, SIDE)
        self.x_first = g % 2 == 0
        self.d = 1 if (g // 2) % 2 == 0 else -1
        self.u, self.v = (x, y) if self.x_first else (y, x)

    def step(self, at, by):
        return lax.rem(at + by + SIDE, SIDE)

    def along_u(self, by):
        u = self.step(self.u, by)
        return {"band": u * SIDE + self.v if self.x_first else self.v * SIDE + u}

    def along_v(self, by):
        v = self.step(self.v, by)
        return {"band": self.u * SIDE + v if self.x_first else v * SIDE + self.u}


def greet():
    barrier = pltpu.get_barrier_semaphore()
    me = lax.axis_index("wave")
    plane = Plane(0)
    for by in (1, -1):
        for where in (plane.along_u(by), plane.along_v(by)):
            pl.semaphore_signal(barrier, inc=1, device_id=where, device_id_type=MESH)
    for d in range(1, WAVES):
        pl.semaphore_signal(
            barrier, inc=1, device_id={"wave": lax.rem(me + d, WAVES)}, device_id_type=MESH
        )
    return barrier, 4 + WAVES - 1


def remote(src, dst, send_sem, recv_sem, where):
    return pltpu.make_async_remote_copy(
        src_ref=src, dst_ref=dst, send_sem=send_sem, recv_sem=recv_sem,
        device_id=where, device_id_type=MESH,
    )


def wave_copies(src, dst, g, send_sem, recv_sem):
    me = lax.axis_index("wave")
    copies = []
    for d in range(1, WAVES):
        peer = lax.rem(me + d, WAVES)
        copies.append(
            remote(src.at[peer, g], dst.at[me, g], send_sem.at[g, d], recv_sem.at[g, d], {"wave": peer})
        )
    return copies


def forward_kernel(
    pairs, spec, leg_hbm, out,
    leg, gath, rows, held, packed, leg_sem, plane_send, plane_recv, wave_send, wave_recv,
):
    me = lax.axis_index("wave")
    barrier, greeted = greet()
    loads = [
        pltpu.make_async_copy(
            leg_hbm.at[pl.ds(GROUP * g, GROUP)], leg.at[pl.ds(GROUP * g, GROUP)], leg_sem.at[g]
        )
        for g in range(GROUPS)
    ]
    planes, hops = [], []
    for g in range(GROUPS):
        p = Plane(g)
        place = (p.u, p.v) if p.x_first else (p.v, p.u)
        gath[g, place[0], place[1]] = jnp.concatenate(
            [spec[TALL * g : TALL * (g + 1), :], jnp.zeros((TALL, 128 - ROWS), BF16)], axis=1
        )

        def one(u, g=g, p=p):
            return gath.at[g, u, p.v] if p.x_first else gath.at[g, p.v, u]

        def line(v, g=g, p=p):
            return gath.at[g, :, v] if p.x_first else gath.at[g, v]

        own, passed = one(p.u), one(p.step(p.u, -p.d))
        full, through = line(p.v), line(p.step(p.v, -p.d))
        plan = (
            (own, p.along_u(1)), (own, p.along_u(-1)), (passed, p.along_u(p.d)),
            (full, p.along_v(1)), (full, p.along_v(-1)), (through, p.along_v(p.d)),
        )
        hops.append(
            [remote(r, r, plane_send.at[g, k], plane_recv.at[g, k], w) for k, (r, w) in enumerate(plan)]
        )
        planes.append(p)
    for load in loads:
        load.start()
    pl.semaphore_wait(barrier, greeted)
    for g in range(GROUPS):
        hops[g][0].start()
        hops[g][1].start()

    sent = []

    def multiply(g):
        for b in range(BANDS):
            rows[:, ROWS * b : ROWS * (b + 1)] = gath[g, b // SIDE, b % SIDE].astype(F32)[:, :ROWS]

        def slots(part, _):
            for k in range(4):
                at = part * 4 + k
                s = GROUP * g + at
                pair = pairs[s]
                value = rows[pl.ds(pl.multiple_of(8 * at, 8), 8), :]
                higher, used, sign = row_marks(pair, (8, NROW))
                value = value * used
                low = jnp.where(higher, 0.0, value) * jnp.where(pair == 0, 1.0, 2.0)
                high = jnp.where(higher, value, 0.0) * 2.0
                x = jnp.concatenate([low, low * sign, high, high * sign], axis=0).astype(BF16)
                held[pl.ds(pl.multiple_of(BAND_LATS * at, 16), BAND_LATS), 0:32] = lax.dot_general(
                    leg[s], x, NT, preferred_element_type=F32
                )
            return 0

        lax.fori_loop(0, GROUP // 4, slots, 0)
        for w in range(WAVES):
            part = [held[pl.ds(LATS * w + i, GROUP, stride=BAND_LATS), :][:, 0:32] for i in range(LATS)]
            first = jnp.concatenate(part[:4], axis=1)
            second = jnp.concatenate([part[4], jnp.zeros((GROUP, 96), F32)], axis=1)
            packed[w, g] = jnp.concatenate([first, second], axis=0).astype(BF16)
        copies = wave_copies(packed, out, g, wave_send, wave_recv)
        for copy in copies:
            copy.start()
        out[me, g] = packed[me, g]
        sent.extend(copies)

    for t in range(GROUPS + 3):
        g = t - 2
        if 0 <= g < GROUPS:
            hops[g][3 if planes[g].d == 1 else 4].wait_recv()
            hops[g][5].start()
        g = t - 1
        if 0 <= g < GROUPS:
            hops[g][1 if planes[g].d == 1 else 0].wait_recv()
            hops[g][2].wait_recv()
            hops[g][3].start()
            hops[g][4].start()
        g = t
        if 0 <= g < GROUPS:
            hops[g][0 if planes[g].d == 1 else 1].wait_recv()
            hops[g][2].start()
        g = t - 3
        if 0 <= g < GROUPS:
            hops[g][4 if planes[g].d == 1 else 3].wait_recv()
            hops[g][5].wait_recv()
            loads[g].wait()
            multiply(g)
    for group in hops:
        for hop in group:
            hop.wait_send()
    for copy in sent:
        copy.wait()


def forward(pairs, spec, leg):
    return pl.pallas_call(
        forward_kernel,
        out_shape=jax.ShapeDtypeStruct((WAVES, GROUPS, 16, 128), BF16),
        in_specs=[
            pl.BlockSpec(memory_space=pltpu.SMEM),
            pl.BlockSpec(memory_space=pltpu.VMEM),
            pl.BlockSpec(memory_space=pl.ANY),
        ],
        out_specs=pl.BlockSpec(memory_space=pltpu.VMEM),
        scratch_shapes=[
            pltpu.VMEM((SLOTS, BAND_LATS, NROW), BF16),
            pltpu.VMEM((GROUPS, SIDE, SIDE, TALL, 128), BF16),
            pltpu.VMEM((TALL, NROW), F32),
            pltpu.VMEM((GROUP * BAND_LATS, 128), F32),
            pltpu.VMEM((WAVES, GROUPS, 16, 128), BF16),
            pltpu.SemaphoreType.DMA((GROUPS,)),
            pltpu.SemaphoreType.DMA((GROUPS, 6)),
            pltpu.SemaphoreType.DMA((GROUPS, 6)),
            pltpu.SemaphoreType.DMA((GROUPS, WAVES)),
            pltpu.SemaphoreType.DMA((GROUPS, WAVES)),
        ],
        compiler_params=pltpu.CompilerParams(
            collective_id=1, has_side_effects=True, vmem_limit_bytes=VMEM_LIMIT
        ),
    )(pairs, spec, leg)


def backward_kernel(
    pairs, coef, leg_hbm, out,
    leg, recv, held, tall, part, first, relay, line, line_out, second, relay_out,
    leg_sem, wave_send, wave_recv, plane_send, plane_recv,
):
    me = lax.axis_index("wave")
    barrier, greeted = greet()
    loads = [
        pltpu.make_async_copy(
            leg_hbm.at[pl.ds(GROUP * g, GROUP)], leg.at[pl.ds(GROUP * g, GROUP)], leg_sem.at[g]
        )
        for g in range(GROUPS)
    ]
    for load in loads:
        load.start()
    planes, hops = [], []
    for g in range(GROUPS):
        p = Plane(g)

        def towards(u, g=g, p=p):
            return part.at[g, u] if p.x_first else part.at[g, :, u]

        plan = (
            (towards(p.step(p.u, 2)), first.at[g, 0], p.along_u(p.d)),
            (towards(p.step(p.u, -p.d)), first.at[g, 1], p.along_u(-p.d)),
            (relay.at[g], first.at[g, 2], p.along_u(p.d)),
            (line_out.at[g, p.step(p.v, 2)], second.at[g, 0], p.along_v(p.d)),
            (line_out.at[g, p.step(p.v, -p.d)], second.at[g, 1], p.along_v(-p.d)),
            (relay_out.at[g], second.at[g, 2], p.along_v(p.d)),
        )
        hops.append(
            [
                remote(a, b, plane_send.at[g, k], plane_recv.at[g, k], w)
                for k, (a, b, w) in enumerate(plan)
            ]
        )
        planes.append(p)
    pl.semaphore_wait(barrier, greeted)
    waves = [wave_copies(coef, recv, g, wave_send, wave_recv) for g in range(GROUPS)]
    for copies in waves:
        for copy in copies:
            copy.start()
    recv[me] = coef[me]

    def mine(g, u):
        return (part[g, u] if planes[g].x_first else part[g, :, u]).astype(F32)

    def multiply(g):
        for w in range(WAVES):
            block = recv[w, g].astype(F32)
            for i in range(LATS):
                value = block[8:16] if i == 4 else block[0:8]
                if 0 < i < 4:
                    value = pltpu.roll(value, 128 - 32 * i, 1)
                held[pl.ds(LATS * w + i, GROUP, stride=BAND_LATS), :] = value

        def slots(piece, _):
            for k in range(4):
                at = piece * 4 + k
                s = GROUP * g + at
                lats = held[pl.ds(pl.multiple_of(BAND_LATS * at, 16), BAND_LATS), :][:, 0:32]
                both = lax.dot_general(lats.astype(BF16), leg[s], TN, preferred_element_type=F32)
                higher, used, sign = row_marks(pairs[s], (8, NROW))
                low = both[0:8] + sign * both[8:16]
                high = both[16:24] + sign * both[24:32]
                tall[pl.ds(pl.multiple_of(8 * at, 8), 8), :] = jnp.where(higher, high, low) * used
            return 0

        lax.fori_loop(0, GROUP // 4, slots, 0)
        for b in range(BANDS):
            part[g, b // SIDE, b % SIDE] = jnp.concatenate(
                [tall[:, ROWS * b : ROWS * (b + 1)], jnp.zeros((TALL, 128 - ROWS), F32)], axis=1
            ).astype(BF16)

    for t in range(GROUPS + 4):
        g = t
        if 0 <= g < GROUPS:
            for copy in waves[g]:
                copy.wait_recv()
            loads[g].wait()
            multiply(g)
            hops[g][0].start()
            hops[g][1].start()
        g = t - 1
        if 0 <= g < GROUPS:
            p = planes[g]
            hops[g][0].wait_recv()
            relay[g] = (first[g, 0].astype(F32) + mine(g, p.step(p.u, p.d))).astype(BF16)
            hops[g][2].start()
        g = t - 2
        if 0 <= g < GROUPS:
            p = planes[g]
            hops[g][1].wait_recv()
            hops[g][2].wait_recv()
            line[g] = mine(g, p.u) + first[g, 1].astype(F32) + first[g, 2].astype(F32)
            line_out[g] = line[g].astype(BF16)
            hops[g][3].start()
            hops[g][4].start()
        g = t - 3
        if 0 <= g < GROUPS:
            p = planes[g]
            hops[g][3].wait_recv()
            relay_out[g] = (second[g, 0].astype(F32) + line[g, p.step(p.v, p.d)]).astype(BF16)
            hops[g][5].start()
        g = t - 4
        if 0 <= g < GROUPS:
            p = planes[g]
            hops[g][4].wait_recv()
            hops[g][5].wait_recv()
            out[TALL * g : TALL * (g + 1), :] = (
                line[g, p.v] + second[g, 1].astype(F32) + second[g, 2].astype(F32)
            ).astype(BF16)
    for group in hops:
        for hop in group:
            hop.wait_send()
    for copies in waves:
        for copy in copies:
            copy.wait_send()


def backward(pairs, coef, leg):
    return pl.pallas_call(
        backward_kernel,
        out_shape=jax.ShapeDtypeStruct((8 * SLOTS, 128), BF16),
        in_specs=[
            pl.BlockSpec(memory_space=pltpu.SMEM),
            pl.BlockSpec(memory_space=pltpu.VMEM),
            pl.BlockSpec(memory_space=pl.ANY),
        ],
        out_specs=pl.BlockSpec(memory_space=pltpu.VMEM),
        scratch_shapes=[
            pltpu.VMEM((SLOTS, BAND_LATS, NROW), BF16),
            pltpu.VMEM((WAVES, GROUPS, 16, 128), BF16),
            pltpu.VMEM((GROUP * BAND_LATS, 128), F32),
            pltpu.VMEM((TALL, NROW), F32),
            pltpu.VMEM((GROUPS, SIDE, SIDE, TALL, 128), BF16),
            pltpu.VMEM((GROUPS, 3, SIDE, TALL, 128), BF16),
            pltpu.VMEM((GROUPS, SIDE, TALL, 128), BF16),
            pltpu.VMEM((GROUPS, SIDE, TALL, 128), F32),
            pltpu.VMEM((GROUPS, SIDE, TALL, 128), BF16),
            pltpu.VMEM((GROUPS, 3, TALL, 128), BF16),
            pltpu.VMEM((GROUPS, TALL, 128), BF16),
            pltpu.SemaphoreType.DMA((GROUPS,)),
            pltpu.SemaphoreType.DMA((GROUPS, WAVES)),
            pltpu.SemaphoreType.DMA((GROUPS, WAVES)),
            pltpu.SemaphoreType.DMA((GROUPS, 6)),
            pltpu.SemaphoreType.DMA((GROUPS, 6)),
        ],
        compiler_params=pltpu.CompilerParams(
            collective_id=2, has_side_effects=True, vmem_limit_bytes=VMEM_LIMIT
        ),
    )(pairs, coef, leg)


def to_grid_kernel(place, four, phase, dft, sel, grid, by_pair, mixed, send_sem, recv_sem):
    rank = lax.axis_index("band") * WAVES + lax.axis_index("wave")
    total = BANDS * WAVES
    ends = (lax.rem(rank + 1, total), lax.rem(rank + total - 1, total))
    ids = [{"band": r // WAVES, "wave": lax.rem(r, WAVES)} for r in ends]
    barrier = pltpu.get_barrier_semaphore()
    for where in ids:
        pl.semaphore_signal(barrier, inc=1, device_id=where, device_id_type=MESH)
    row = lax.broadcasted_iota(jnp.int32, (640, 640), 0)
    onehot = jnp.where(row == place[...], 1.0, 0.0).astype(BF16)
    blocks = four[...].astype(F32)
    slots = jnp.concatenate(
        [blocks[:, :, 0:8].reshape(640, 128), blocks[:, :, 8:16].reshape(640, 128)], axis=1
    ).astype(BF16)
    ordered = jnp.dot(onehot, slots, preferred_element_type=F32).astype(BF16)
    by_pair[...] = jnp.dot(ordered, sel[...], preferred_element_type=F32).astype(BF16)
    for m1 in range(M1):
        low, high = pl.ds(P2 * m1, P2), pl.ds(P2 * (M1 - 1 - m1), P2)
        left = jnp.concatenate(
            [by_pair[low, 0:128], by_pair[low, 128:256], by_pair[high, 256:384], by_pair[high, 384:512]],
            axis=0,
        )
        part = lax.dot_general(left, phase[64 * m1 : 64 * m1 + 64, :], TN, preferred_element_type=F32)
        mixed[pl.ds(m1, 40, stride=M1), :] = part[0:40, 0:128]
        mixed[pl.ds(1600 + m1, 40, stride=M1), :] = part[0:40, 128:256]
    for n in range(LATS * FIELDS):
        right = jnp.concatenate(
            [mixed[80 * n : 80 * n + 80, :], mixed[1600 + 80 * n : 1680 + 80 * n, :]], axis=0
        ).astype(BF16)
        grid[RIM + n // FIELDS, n % FIELDS] = jnp.dot(
            dft[...], right, preferred_element_type=F32
        ).astype(BF16)
    pl.semaphore_wait(barrier, 2)
    copies = [
        remote(grid.at[pl.ds(a, RIM)], grid.at[pl.ds(b, RIM)], send_sem.at[k], recv_sem.at[k], ids[k])
        for k, (a, b) in enumerate(((LATS, 0), (RIM, RIM + LATS)))
    ]
    for copy in copies:
        copy.start()
    for copy in copies:
        copy.wait()


def whole(n):
    return [pl.BlockSpec(memory_space=pltpu.VMEM)] * n


def to_grid(place, four, phase, dft, sel):
    return pl.pallas_call(
        to_grid_kernel,
        out_shape=jax.ShapeDtypeStruct((LATS + 2 * RIM, FIELDS, 80, Q2), BF16),
        in_specs=whole(5),
        out_specs=whole(1)[0],
        scratch_shapes=[
            pltpu.VMEM((640, 512), BF16),
            pltpu.VMEM((3200, 128), F32),
            pltpu.SemaphoreType.DMA((2,)),
            pltpu.SemaphoreType.DMA((2,)),
        ],
        compiler_params=pltpu.CompilerParams(
            collective_id=3, has_side_effects=True, vmem_limit_bytes=VMEM_LIMIT
        ),
    )(place, four, phase, dft, sel)


def shifted(x, by, lane):
    if by == 0:
        return x
    if by > 0:
        carried = jnp.concatenate([x[2:], x[:2]], axis=0)
        return pltpu.roll(jnp.where(lane < by, carried, x), Q2 - by, 1)
    carried = jnp.concatenate([x[78:], x[:78]], axis=0)
    return pltpu.roll(jnp.where(lane >= Q2 + by, carried, x), -by, 1)


def spread(values, bit, step):
    n = len(values)
    out = []
    for k in range(n + step):
        keep = values[k] if k < n else 0.0
        moved = values[k - step] if k >= step else 0.0
        out.append(jnp.where(bit, moved, keep))
    return out


def stencil_kernel(
    rank, grid, code, pick, weight, quad, place, phase, dft_back, sel_back,
    arrival, back, ext, moved, summed, mixed, by_pair,
):
    lane = lax.broadcasted_iota(jnp.int32, (80, Q2), 1)
    row_odd = (lax.broadcasted_iota(jnp.int32, (80, Q2), 0) & 1) == 1
    for f in range(FIELDS):
        for i in range(LATS):
            ext[RIM + i, f] = grid[RIM + i, f].astype(F32)
        for k in range(RIM):
            ext[k, f] = grid[k, f].astype(F32)
            ext[RIM + LATS + k, f] = grid[RIM + LATS + k, f].astype(F32)

    @pl.when(rank[0] == 0)
    def _():
        for f in range(FIELDS):
            for k in range(RIM):
                x = grid[2 * RIM - 1 - k, f].astype(F32)
                ext[k, f] = jnp.concatenate([x[40:], x[:40]], axis=0)

    @pl.when(rank[0] == BANDS * WAVES - 1)
    def _():
        for f in range(FIELDS):
            for k in range(RIM):
                x = grid[RIM + LATS - 1 - k, f].astype(F32)
                up = jnp.concatenate([x[1:], x[:1]], axis=0)
                down = jnp.concatenate([x[79:], x[:79]], axis=0)
                ext[RIM + LATS + k, f] = jnp.where(row_odd, down, up)

    def shift_row(n, _):
        x = ext[n // FIELDS, lax.rem(n, FIELDS)]
        for c in range(7):
            moved[c, n // FIELDS, lax.rem(n, FIELDS)] = shifted(x, c - 3, lane)
        return 0

    lax.fori_loop(0, (LATS + 2 * RIM) * FIELDS, shift_row, 0)

    def chunk(n, _):
        i, start = n // 10, pl.multiple_of(lax.rem(n, 10) * 8, 8)
        at = pl.multiple_of(n * 8, 8)
        e = code[pl.ds(at, 8), :]
        t = pick[pl.ds(at, 8), :]
        taps = [
            jnp.take_along_axis(jnp.broadcast_to(weight[k : k + 1, :], (8, 128)), t, axis=1)
            for k in range(16)
        ]
        x0, x1 = (e & 1) == 1, (e & 2) == 2
        y0, y1 = (e & 4) == 4, (e & 8) == 8
        columns = [spread([taps[4 * a + b] for a in range(4)], y0, 1) for b in range(4)]
        columns = [spread(column, y1, 2) for column in columns]
        total = [jnp.zeros((8, 128), F32) for _ in range(FIELDS)]
        for sr in range(7):
            factors = spread(spread([columns[b][sr] for b in range(4)], x0, 1), x1, 2)
            for sc in range(7):
                for f in range(FIELDS):
                    total[f] = total[f] + factors[sc] * moved[sc, i + sr, f, pl.ds(start, 8), :]
        for f in range(FIELDS):
            summed[i, f, pl.ds(start, 8), :] = total[f]
        return 0

    lax.fori_loop(0, 50, chunk, 0)
    for n in range(LATS * FIELDS):
        i, f = n // FIELDS, n % FIELDS
        value = summed[i, f].astype(BF16)
        arrival[f, 80 * i : 80 * i + 80, :] = value
        both = jnp.dot(dft_back[...], value, preferred_element_type=F32)
        mixed[80 * n : 80 * n + 80, :] = both[0:80]
        mixed[1600 + 80 * n : 1680 + 80 * n, :] = both[80:160]
    by_pair[...] = jnp.zeros((640, 512), BF16)
    for m1 in range(M1):
        right = jnp.concatenate(
            [mixed[pl.ds(m1, 40, stride=M1), :], mixed[pl.ds(1600 + m1, 40, stride=M1), :]], axis=1
        ).astype(BF16)
        part = lax.dot_general(phase[64 * m1 : 64 * m1 + 64, :], right, NT, preferred_element_type=F32)
        part = (part * quad[:, 0:40]).astype(BF16)
        low, high = pl.ds(P2 * m1, P2), pl.ds(P2 * (M1 - 1 - m1), P2)
        for k, where in enumerate((low, low, high, high)):
            by_pair[where, 128 * k : 128 * k + 40] = part[16 * k : 16 * k + 16]
    ordered = jnp.dot(by_pair[...], sel_back[...], preferred_element_type=F32).astype(BF16)
    column = lax.broadcasted_iota(jnp.int32, (640, 640), 1)
    onehot = jnp.where(column == place[...], 1.0, 0.0).astype(BF16)
    slots = jnp.dot(onehot, ordered, preferred_element_type=F32)
    back[...] = jnp.concatenate(
        [slots[:, 0:128].reshape(80, 8, 128), slots[:, 128:256].reshape(80, 8, 128)], axis=1
    ).astype(BF16).reshape(WAVES, GROUPS, 16, 128)


def stencil(rank, grid, code, pick, weight, quad, place, phase, dft_back, sel_back):
    return pl.pallas_call(
        stencil_kernel,
        out_shape=(
            jax.ShapeDtypeStruct((FIELDS, 2 * LATS * Q1, Q2), BF16),
            jax.ShapeDtypeStruct((WAVES, GROUPS, 16, 128), BF16),
        ),
        in_specs=[pl.BlockSpec(memory_space=pltpu.SMEM)] + whole(9),
        out_specs=tuple(whole(2)),
        scratch_shapes=[
            pltpu.VMEM((LATS + 2 * RIM, FIELDS, 80, Q2), F32),
            pltpu.VMEM((7, LATS + 2 * RIM, FIELDS, 80, Q2), F32),
            pltpu.VMEM((LATS, FIELDS, 80, Q2), F32),
            pltpu.VMEM((3200, 128), F32),
            pltpu.VMEM((640, 512), BF16),
        ],
        compiler_params=pltpu.CompilerParams(vmem_limit_bytes=VMEM_LIMIT),
    )(rank, grid, code, pick, weight, quad, place, phase, dft_back, sel_back)


def grid_view(x):
    return x.reshape(2, LATS, Q1, Q2).transpose(1, 2, 0, 3).reshape(2 * LATS * Q1, Q2)


def per_device(
    spectral, legendre, slot_pair, quad_weight, depart_code, stencil_pick, stencil_weight
):
    phase, dft, dft_back, sel, sel_back = [jnp.asarray(t) for t in phase_tables()]
    wave_rank = lax.axis_index("wave")
    band_rank = lax.axis_index("band")
    pairs = lax.dynamic_slice_in_dim(slot_pair, wave_rank * SLOTS, SLOTS)
    place = (slot_pair % M1) * P2 + slot_pair // M1
    rank = (band_rank * WAVES + wave_rank).reshape(1)
    my_weight = lax.dynamic_slice_in_dim(quad_weight, wave_rank * LATS, LATS)
    quad = jnp.repeat(my_weight / math.sqrt(NLON), 2 * FIELDS)
    quad = jnp.pad(quad, (0, 128 - quad.shape[0])).reshape(1, 128)
    weight = jnp.pad(stencil_weight.T, ((0, 0), (0, 112)))

    own = spectral.transpose(0, 2, 1).reshape(8 * SLOTS, ROWS)
    four = forward(pairs, own, legendre)
    grid = to_grid(place.reshape(1, -1), four, phase, dft, sel)
    arrival, back = stencil(
        rank, grid, grid_view(depart_code), grid_view(stencil_pick), weight, quad,
        place.reshape(-1, 1), phase, dft_back, sel_back,
    )
    total = backward(pairs, back, legendre)
    spectral_out = total.reshape(SLOTS, 8, 128)[:, :, :ROWS].transpose(0, 2, 1)
    arrival = arrival.reshape(FIELDS, LATS, Q1, 2, Q2).transpose(0, 3, 1, 2, 4)
    return arrival.reshape(1, FIELDS, 2, LATS, NLON), spectral_out


def solution(mesh):
    lat = ("band", "wave")
    in_specs = (
        P("wave", "band", None),
        P("wave", "band", None),
        P(),
        P("band"),
        P(None, None, lat, None),
        P(None, None, lat, None),
        P(),
    )
    out_specs = (P(None, None, None, lat, None), P("wave", "band", None))
    return jax.shard_map(
        per_device, mesh=mesh, in_specs=in_specs, out_specs=out_specs, check_vma=False
    )
```

time: 147 us -> 115 us (0.78)
  the two profiles are of different devices: /device:TPU:1 before, /device:TPU:8 now
where the time goes in v2:
time: 115 us
  Pallas kernels  109 us (95%)
  local copies, waits for them, and re-layouts  3.55 us (3%)
  other arithmetic  1.43 us (1%)
    pallas_call x1, Pallas kernels, forward(): pl.pallas_call(forward_kernel, out_shape=jax.ShapeDtypeStruct((WAVES, GRO...  47.3 us
    pallas_call x1, Pallas kernels, backward(): pl.pallas_call(backward_kernel, out_shape=jax.ShapeDtypeStruct((8 * SLOTS...  38.6 us
    pallas_call x1, Pallas kernels, stencil(): pl.pallas_call(stencil_kernel, out_shape=(jax.ShapeDtypeStruct((FIELDS, 2...  15.3 us
    pallas_call x1, Pallas kernels, to_grid(): pl.pallas_call(to_grid_kernel, out_shape=jax.ShapeDtypeStruct((LATS + 2 *...  7.94 us

profile of v2, /device:TPU:8, one launch (start us, length us, event | category | flops | bytes accessed | tf_op | source)
XLA Modules:
  0.0 114.9 jit_solution(11215057761443672421)
XLA Ops:
  0.6 0.0 copy-start
  0.6 0.0 copy-start.2
  0.7 0.0 copy-start.1
  0.7 0.0 copy-start.4
  0.7 0.0 copy-start.3
  0.7 0.9 dynamic_slice.6.pairs
  1.6 0.7 dynamic-slice_multiply_fusion
  2.3 0.1 broadcast_in_dim.3
  2.4 0.1 reshape.50
  2.5 0.7 fusion.1
  3.2 0.8 copy.20
  4.0 0.1 reshape.56.place
  4.1 0.0 copy-start.5
  4.1 0.9 copy-done.5
  5.0 47.3 %shard_map.131.four = bf16[16,5,16,128]{3,2,1,0:T(8,128)(2,1)S(1)} custom-call(s32[40]{0:T(128)S(1)} %dynamic_slice.6.pairs, bf16[320,88]{1,0:T(8,128)(2,1)S(1)} %bitcast.28, bf16[40,80,1408]{2,1,0:T(8,128)(2,1)} %leg_hbm.3), custom_call_target="tpu_custom_call" | custom-call | tf_op jit(solution)/shard_map/pallas_call | solution.py:241
  52.3 0.0 copy-done
  52.4 0.0 copy-done.2
  52.4 0.0 copy-done.7
  52.4 7.9 %shard_map.132.grid = bf16[11,4,80,128]{3,2,1,0:T(8,128)(2,1)S(1)} custom-call(s32[1,640]{1,0:T(1,128)S(1)} %reshape.44.place, bf16[16,5,16,128]{3,2,1,0:T(8,128)(2,1)S(1)} %shard_map.131.four, bf16[2560,256]{1,0:T(8,128)(2,1)S(1)} %copy-done, bf16[80,160]{1,0:T(8,128)(2,1)S(1)} %copy-done.7, bf16[256,512]{1,0:T(8,128)(2,1)S(1)} %copy-done.2), custom_call_target="tpu_custom_call" | custom-call | tf_op jit(solution)/shard_map/pallas_call | solution.py:470
  60.3 0.0 copy-done.1
  60.3 0.0 copy-done.4
  60.4 15.3 %shard_map.133 = (bf16[4,400,128]{2,1,0:T(8,128)(2,1)}, bf16[16,5,16,128]{3,2,1,0:T(8,128)(2,1)S(1)}) custom-call(s32[1]{0:T(128)} %bitcast.rank, bf16[11,4,80,128]{3,2,1,0:T(8,128)(2,1)S(1)} %shard_map.132.grid, s32[400,128]{1,0:T(8,128)S(1)} %bitcast.26, s32[400,128]{1,0:T(8,128)S(1)} %bitcast.27, f32[16,128]{1,0:T(8,128)S(1)} %pad.8.weight, ...), custom_call_target="tpu_custom_call" | custom-call | tf_op jit(solution)/shard_map/pallas_call | solution.py:595
  75.6 38.6 %shard_map.134 = bf16[320,128]{1,0:T(8,128)(2,1)S(1)} custom-call(s32[40]{0:T(128)S(1)} %dynamic_slice.6.pairs, bf16[16,5,16,128]{3,2,1,0:T(8,128)(2,1)S(1)} %get-tuple-element.5.coef, bf16[40,80,1408]{2,1,0:T(8,128)(2,1)} %leg_hbm.3), custom_call_target="tpu_custom_call" | custom-call | tf_op jit(solution)/shard_map/pallas_call | solution.py:389
  114.3 0.6 slice_bitcast_fusion
  (7 shorter events, 0.0 us)
Async XLA Ops:
  0.6 51.7 %copy-start = (bf16[2560,256]{1,0:T(8,128)(2,1)S(1)}, bf16[2560,256]{1,0:T(8,128)(2,1)}, u32[]{:S(2)}) copy-start(bf16[2560,256]{1,0:T(8,128)(2,1)} %constant.52.clone.phase) | copy-start | bytes 3932164
  0.6 51.7 %copy-start.2 = (bf16[256,512]{1,0:T(8,128)(2,1)S(1)}, bf16[256,512]{1,0:T(8,128)(2,1)}, u32[]{:S(2)}) copy-start(bf16[256,512]{1,0:T(8,128)(2,1)} %constant.55.clone.sel) | copy-start | bytes 786436
  0.7 59.7 %copy-start.1 = (bf16[512,256]{1,0:T(8,128)(2,1)S(1)}, bf16[512,256]{1,0:T(8,128)(2,1)}, u32[]{:S(2)}) copy-start(bf16[512,256]{1,0:T(8,128)(2,1)} %constant.56.clone.sel_back) | copy-start | bytes 786436
  0.7 59.7 %copy-start.4 = (s32[1,2,5,5120]{3,1,2,0:T(2,128)S(1)}, s32[1,2,5,5120]{3,1,2,0:T(2,128)}, u32[]{:S(2)}) copy-start(s32[1,2,5,5120]{3,1,2,0:T(2,128)} %param.17) | copy-start | bytes 614404
  0.7 59.7 %copy-start.3 = (s32[1,2,5,5120]{3,1,2,0:T(2,128)S(1)}, s32[1,2,5,5120]{3,1,2,0:T(2,128)}, u32[]{:S(2)}) copy-start(s32[1,2,5,5120]{3,1,2,0:T(2,128)} %param.16) | copy-start | bytes 614404
  4.1 0.9 copy-start.5
  5.0 47.3 %copy-start.7 = (bf16[80,160]{1,0:T(8,128)(2,1)S(1)}, bf16[80,160]{1,0:T(8,128)(2,1)}, u32[]{:S(2)}) copy-start(bf16[80,160]{1,0:T(8,128)(2,1)} %constant.53.clone.dft) | copy-start | bytes 76804
  5.0 55.3 %copy-start.6 = (bf16[160,80]{1,0:T(8,128)(2,1)S(1)}, bf16[160,80]{1,0:T(8,128)(2,1)}, u32[]{:S(2)}) copy-start(bf16[160,80]{1,0:T(8,128)(2,1)} %constant.54.clone.dft_back) | copy-start | bytes 76804

commit v3 on v2

--- a/solution.py
+++ b/solution.py
@@ -68,6 +68,8 @@
 GROUPS = 5
 GROUP = SLOTS // GROUPS
 TALL = 8 * GROUP
+HALF = TALL // 2
+STEPS = (1, 3, 2)
 SIDE = 4
 
 
@@ -81,37 +83,37 @@
 
 
 class Plane:
-    def __init__(self, g):
+    def __init__(self, k):
         band = lax.axis_index("band")
         x, y = band // SIDE, lax.rem(band, SIDE)
-        self.x_first = g % 2 == 0
-        self.d = 1 if (g // 2) % 2 == 0 else -1
+        self.x_first = k == 0
         self.u, self.v = (x, y) if self.x_first else (y, x)
 
-    def step(self, at, by):
-        return lax.rem(at + by + SIDE, SIDE)
-
     def along_u(self, by):
-        u = self.step(self.u, by)
+        u = turn(self.u, by)
         return {"band": u * SIDE + self.v if self.x_first else self.v * SIDE + u}
 
     def along_v(self, by):
-        v = self.step(self.v, by)
+        v = turn(self.v, by)
         return {"band": self.u * SIDE + v if self.x_first else v * SIDE + self.u}
+
+
+def turn(at, by):
+    return lax.rem(at + by, SIDE)
 
 
 def greet():
     barrier = pltpu.get_barrier_semaphore()
     me = lax.axis_index("wave")
     plane = Plane(0)
-    for by in (1, -1):
+    for by in (1, 3, 2):
         for where in (plane.along_u(by), plane.along_v(by)):
             pl.semaphore_signal(barrier, inc=1, device_id=where, device_id_type=MESH)
     for d in range(1, WAVES):
         pl.semaphore_signal(
             barrier, inc=1, device_id={"wave": lax.rem(me + d, WAVES)}, device_id_type=MESH
         )
-    return barrier, 4 + WAVES - 1
+    return barrier, 6 + WAVES - 1
 
 
 def remote(src, dst, send_sem, recv_sem, where):
@@ -144,48 +146,49 @@
         )
         for g in range(GROUPS)
     ]
-    planes, hops = [], []
+    near, far = [], []
     for g in range(GROUPS):
-        p = Plane(g)
-        place = (p.u, p.v) if p.x_first else (p.v, p.u)
-        gath[g, place[0], place[1]] = jnp.concatenate(
-            [spec[TALL * g : TALL * (g + 1), :], jnp.zeros((TALL, 128 - ROWS), BF16)], axis=1
-        )
-
-        def one(u, g=g, p=p):
-            return gath.at[g, u, p.v] if p.x_first else gath.at[g, p.v, u]
-
-        def line(v, g=g, p=p):
-            return gath.at[g, :, v] if p.x_first else gath.at[g, v]
-
-        own, passed = one(p.u), one(p.step(p.u, -p.d))
-        full, through = line(p.v), line(p.step(p.v, -p.d))
-        plan = (
-            (own, p.along_u(1)), (own, p.along_u(-1)), (passed, p.along_u(p.d)),
-            (full, p.along_v(1)), (full, p.along_v(-1)), (through, p.along_v(p.d)),
-        )
-        hops.append(
-            [remote(r, r, plane_send.at[g, k], plane_recv.at[g, k], w) for k, (r, w) in enumerate(plan)]
-        )
-        planes.append(p)
+        for k in range(2):
+            p = Plane(k)
+            start = TALL * g + HALF * k
+            own = jnp.concatenate(
+                [spec[start : start + HALF, :], jnp.zeros((HALF, 128 - ROWS), BF16)], axis=1
+            )
+            if k == 0:
+                gath[g, 0, p.u, p.v] = own
+                one, line = gath.at[g, 0, p.u, p.v], gath.at[g, 0, :, p.v]
+            else:
+                gath[g, 1, p.v, p.u] = own
+                one, line = gath.at[g, 1, p.v, p.u], gath.at[g, 1, p.v]
+            for n, by in enumerate(STEPS):
+                near.append(
+                    remote(one, one, plane_send.at[g, k, n], plane_recv.at[g, k, n], p.along_u(by))
+                )
+                far.append(
+                    remote(
+                        line, line, plane_send.at[g, k, 3 + n], plane_recv.at[g, k, 3 + n], p.along_v(by)
+                    )
+                )
+    pl.semaphore_wait(barrier, greeted)
+    for hop in near:
+        hop.start()
     for load in loads:
         load.start()
-    pl.semaphore_wait(barrier, greeted)
-    for g in range(GROUPS):
-        hops[g][0].start()
-        hops[g][1].start()
 
     sent = []
 
     def multiply(g):
         for b in range(BANDS):
-            rows[:, ROWS * b : ROWS * (b + 1)] = gath[g, b // SIDE, b % SIDE].astype(F32)[:, :ROWS]
+            for k in range(2):
+                rows[HALF * k : HALF * (k + 1), ROWS * b : ROWS * (b + 1)] = gath[
+                    g, k, b // SIDE, b % SIDE
+                ].astype(F32)[:, :ROWS]
 
         def slots(part, _):
             for k in range(4):
                 at = part * 4 + k
                 s = GROUP * g + at
-                pair = pairs[s]
+                pair = pairs[me * SLOTS + s]
                 value = rows[pl.ds(pl.multiple_of(8 * at, 8), 8), :]
                 higher, used, sign = row_marks(pair, (8, NROW))
                 value = value * used
@@ -209,30 +212,18 @@
         out[me, g] = packed[me, g]
         sent.extend(copies)
 
-    for t in range(GROUPS + 3):
-        g = t - 2
-        if 0 <= g < GROUPS:
-            hops[g][3 if planes[g].d == 1 else 4].wait_recv()
-            hops[g][5].start()
-        g = t - 1
-        if 0 <= g < GROUPS:
-            hops[g][1 if planes[g].d == 1 else 0].wait_recv()
-            hops[g][2].wait_recv()
-            hops[g][3].start()
-            hops[g][4].start()
-        g = t
-        if 0 <= g < GROUPS:
-            hops[g][0 if planes[g].d == 1 else 1].wait_recv()
-            hops[g][2].start()
-        g = t - 3
-        if 0 <= g < GROUPS:
-            hops[g][4 if planes[g].d == 1 else 3].wait_recv()
-            hops[g][5].wait_recv()
-            loads[g].wait()
-            multiply(g)
-    for group in hops:
-        for hop in group:
-            hop.wait_send()
+    for g in range(GROUPS):
+        for k in range(6):
+            near[6 * g + k].wait_recv()
+        for k in range(6):
+            far[6 * g + k].start()
+    for g in range(GROUPS):
+        for k in range(6):
+            far[6 * g + k].wait_recv()
+        loads[g].wait()
+        multiply(g)
+    for hop in near + far:
+        hop.wait_send()
     for copy in sent:
         copy.wait()
 
@@ -249,13 +240,13 @@
         out_specs=pl.BlockSpec(memory_space=pltpu.VMEM),
         scratch_shapes=[
             pltpu.VMEM((SLOTS, BAND_LATS, NROW), BF16),
-            pltpu.VMEM((GROUPS, SIDE, SIDE, TALL, 128), BF16),
+            pltpu.VMEM((GROUPS, 2, SIDE, SIDE, HALF, 128), BF16),
             pltpu.VMEM((TALL, NROW), F32),
             pltpu.VMEM((GROUP * BAND_LATS, 128), F32),
             pltpu.VMEM((WAVES, GROUPS, 16, 128), BF16),
             pltpu.SemaphoreType.DMA((GROUPS,)),
-            pltpu.SemaphoreType.DMA((GROUPS, 6)),
-            pltpu.SemaphoreType.DMA((GROUPS, 6)),
+            pltpu.SemaphoreType.DMA((GROUPS, 2, 6)),
+            pltpu.SemaphoreType.DMA((GROUPS, 2, 6)),
             pltpu.SemaphoreType.DMA((GROUPS, WAVES)),
             pltpu.SemaphoreType.DMA((GROUPS, WAVES)),
         ],
@@ -267,7 +258,7 @@
 
 def backward_kernel(
     pairs, coef, leg_hbm, out,
-    leg, recv, held, tall, part, first, relay, line, line_out, second, relay_out,
+    leg, recv, held, tall, part, first, line, line_out, second,
     leg_sem, wave_send, wave_recv, plane_send, plane_recv,
 ):
     me = lax.axis_index("wave")
@@ -280,37 +271,30 @@
     ]
     for load in loads:
         load.start()
-    planes, hops = [], []
+    near, far = [], []
     for g in range(GROUPS):
-        p = Plane(g)
-
-        def towards(u, g=g, p=p):
-            return part.at[g, u] if p.x_first else part.at[g, :, u]
-
-        plan = (
-            (towards(p.step(p.u, 2)), first.at[g, 0], p.along_u(p.d)),
-            (towards(p.step(p.u, -p.d)), first.at[g, 1], p.along_u(-p.d)),
-            (relay.at[g], first.at[g, 2], p.along_u(p.d)),
-            (line_out.at[g, p.step(p.v, 2)], second.at[g, 0], p.along_v(p.d)),
-            (line_out.at[g, p.step(p.v, -p.d)], second.at[g, 1], p.along_v(-p.d)),
-            (relay_out.at[g], second.at[g, 2], p.along_v(p.d)),
-        )
-        hops.append(
-            [
-                remote(a, b, plane_send.at[g, k], plane_recv.at[g, k], w)
-                for k, (a, b, w) in enumerate(plan)
-            ]
-        )
-        planes.append(p)
+        for k in range(2):
+            p = Plane(k)
+            for n, by in enumerate(STEPS):
+                u, v = turn(p.u, by), turn(p.v, by)
+                src = part.at[g, 0, u] if k == 0 else part.at[g, 1, :, u]
+                near.append(
+                    remote(
+                        src, first.at[g, k, n], plane_send.at[g, k, n], plane_recv.at[g, k, n], p.along_u(by)
+                    )
+                )
+                far.append(
+                    remote(
+                        line_out.at[g, k, v], second.at[g, k, n],
+                        plane_send.at[g, k, 3 + n], plane_recv.at[g, k, 3 + n], p.along_v(by),
+                    )
+                )
     pl.semaphore_wait(barrier, greeted)
     waves = [wave_copies(coef, recv, g, wave_send, wave_recv) for g in range(GROUPS)]
     for copies in waves:
         for copy in copies:
             copy.start()
     recv[me] = coef[me]
-
-    def mine(g, u):
-        return (part[g, u] if planes[g].x_first else part[g, :, u]).astype(F32)
 
     def multiply(g):
         for w in range(WAVES):
@@ -327,7 +311,7 @@
                 s = GROUP * g + at
                 lats = held[pl.ds(pl.multiple_of(BAND_LATS * at, 16), BAND_LATS), :][:, 0:32]
                 both = lax.dot_general(lats.astype(BF16), leg[s], TN, preferred_element_type=F32)
-                higher, used, sign = row_marks(pairs[s], (8, NROW))
+                higher, used, sign = row_marks(pairs[me * SLOTS + s], (8, NROW))
                 low = both[0:8] + sign * both[8:16]
                 high = both[16:24] + sign * both[24:32]
                 tall[pl.ds(pl.multiple_of(8 * at, 8), 8), :] = jnp.where(higher, high, low) * used
@@ -335,51 +319,44 @@
 
         lax.fori_loop(0, GROUP // 4, slots, 0)
         for b in range(BANDS):
-            part[g, b // SIDE, b % SIDE] = jnp.concatenate(
+            both = jnp.concatenate(
                 [tall[:, ROWS * b : ROWS * (b + 1)], jnp.zeros((TALL, 128 - ROWS), F32)], axis=1
             ).astype(BF16)
-
-    for t in range(GROUPS + 4):
+            for k in range(2):
+                part[g, k, b // SIDE, b % SIDE] = both[HALF * k : HALF * (k + 1)]
+
+    for t in range(GROUPS + 2):
         g = t
         if 0 <= g < GROUPS:
             for copy in waves[g]:
                 copy.wait_recv()
             loads[g].wait()
             multiply(g)
-            hops[g][0].start()
-            hops[g][1].start()
+            for k in range(6):
+                near[6 * g + k].start()
         g = t - 1
         if 0 <= g < GROUPS:
-            p = planes[g]
-            hops[g][0].wait_recv()
-            relay[g] = (first[g, 0].astype(F32) + mine(g, p.step(p.u, p.d))).astype(BF16)
-            hops[g][2].start()
+            for k in range(2):
+                p = Plane(k)
+                total = (part[g, 0, p.u] if k == 0 else part[g, 1, :, p.u]).astype(F32)
+                for n in range(3):
+                    near[6 * g + 3 * k + n].wait_recv()
+                    total = total + first[g, k, n].astype(F32)
+                line[g, k] = total
+                line_out[g, k] = total.astype(BF16)
+                for n in range(3):
+                    far[6 * g + 3 * k + n].start()
         g = t - 2
         if 0 <= g < GROUPS:
-            p = planes[g]
-            hops[g][1].wait_recv()
-            hops[g][2].wait_recv()
-            line[g] = mine(g, p.u) + first[g, 1].astype(F32) + first[g, 2].astype(F32)
-            line_out[g] = line[g].astype(BF16)
-            hops[g][3].start()
-            hops[g][4].start()
-        g = t - 3
-        if 0 <= g < GROUPS:
-            p = planes[g]
-            hops[g][3].wait_recv()
-            relay_out[g] = (second[g, 0].astype(F32) + line[g, p.step(p.v, p.d)]).astype(BF16)
-            hops[g][5].start()
-        g = t - 4
-        if 0 <= g < GROUPS:
-            p = planes[g]
-            hops[g][4].wait_recv()
-            hops[g][5].wait_recv()
-            out[TALL * g : TALL * (g + 1), :] = (
-                line[g, p.v] + second[g, 1].astype(F32) + second[g, 2].astype(F32)
-            ).astype(BF16)
-    for group in hops:
-        for hop in group:
-            hop.wait_send()
+            for k in range(2):
+                total = line[g, k, Plane(k).v]
+                for n in range(3):
+                    far[6 * g + 3 * k + n].wait_recv()
+                    total = total + second[g, k, n].astype(F32)
+                start = TALL * g + HALF * k
+                out[start : start + HALF, :] = total.astype(BF16)
+    for hop in near + far:
+        hop.wait_send()
     for copies in waves:
         for copy in copies:
             copy.wait_send()
@@ -400,18 +377,16 @@
             pltpu.VMEM((WAVES, GROUPS, 16, 128), BF16),
             pltpu.VMEM((GROUP * BAND_LATS, 128), F32),
             pltpu.VMEM((TALL, NROW), F32),
-            pltpu.VMEM((GROUPS, SIDE, SIDE, TALL, 128), BF16),
-            pltpu.VMEM((GROUPS, 3, SIDE, TALL, 128), BF16),
-            pltpu.VMEM((GROUPS, SIDE, TALL, 128), BF16),
-            pltpu.VMEM((GROUPS, SIDE, TALL, 128), F32),
-            pltpu.VMEM((GROUPS, SIDE, TALL, 128), BF16),
-            pltpu.VMEM((GROUPS, 3, TALL, 128), BF16),
-            pltpu.VMEM((GROUPS, TALL, 128), BF16),
+            pltpu.VMEM((GROUPS, 2, SIDE, SIDE, HALF, 128), BF16),
+            pltpu.VMEM((GROUPS, 2, 3, SIDE, HALF, 128), BF16),
+            pltpu.VMEM((GROUPS, 2, SIDE, HALF, 128), F32),
+            pltpu.VMEM((GROUPS, 2, SIDE, HALF, 128), BF16),
+            pltpu.VMEM((GROUPS, 2, 3, HALF, 128), BF16),
             pltpu.SemaphoreType.DMA((GROUPS,)),
             pltpu.SemaphoreType.DMA((GROUPS, WAVES)),
             pltpu.SemaphoreType.DMA((GROUPS, WAVES)),
-            pltpu.SemaphoreType.DMA((GROUPS, 6)),
-            pltpu.SemaphoreType.DMA((GROUPS, 6)),
+            pltpu.SemaphoreType.DMA((GROUPS, 2, 6)),
+            pltpu.SemaphoreType.DMA((GROUPS, 2, 6)),
         ],
         compiler_params=pltpu.CompilerParams(
             collective_id=2, has_side_effects=True, vmem_limit_bytes=VMEM_LIMIT
@@ -428,7 +403,7 @@
     for where in ids:
         pl.semaphore_signal(barrier, inc=1, device_id=where, device_id_type=MESH)
     row = lax.broadcasted_iota(jnp.int32, (640, 640), 0)
-    onehot = jnp.where(row == place[...], 1.0, 0.0).astype(BF16)
+    onehot = jnp.where(row == order_of(place[...]), 1.0, 0.0).astype(BF16)
     blocks = four[...].astype(F32)
     slots = jnp.concatenate(
         [blocks[:, :, 0:8].reshape(640, 128), blocks[:, :, 8:16].reshape(640, 128)], axis=1
@@ -462,6 +437,11 @@
         copy.wait()
 
 
+def order_of(pair):
+    p2 = (pair * 1639) >> 16
+    return (pair - M1 * p2) * P2 + p2
+
+
 def whole(n):
     return [pl.BlockSpec(memory_space=pltpu.VMEM)] * n
 
@@ -484,16 +464,6 @@
     )(place, four, phase, dft, sel)
 
 
-def shifted(x, by, lane):
-    if by == 0:
-        return x
-    if by > 0:
-        carried = jnp.concatenate([x[2:], x[:2]], axis=0)
-        return pltpu.roll(jnp.where(lane < by, carried, x), Q2 - by, 1)
-    carried = jnp.concatenate([x[78:], x[:78]], axis=0)
-    return pltpu.roll(jnp.where(lane >= Q2 + by, carried, x), -by, 1)
-
-
 def spread(values, bit, step):
     n = len(values)
     out = []
@@ -506,9 +476,15 @@
 
 def stencil_kernel(
     rank, grid, code, pick, weight, quad, place, phase, dft_back, sel_back,
-    arrival, back, ext, moved, summed, mixed, by_pair,
+    arrival, back, ext, moved, summed, mixed, by_pair, taps_of, shifts, shifts2,
 ):
-    lane = lax.broadcasted_iota(jnp.int32, (80, Q2), 1)
+    wave = lax.axis_index("wave")
+    lat = lax.broadcasted_iota(jnp.int32, (1, 40), 1) // (2 * FIELDS)
+    scale = jnp.zeros((1, 40), F32)
+    for i in range(LATS):
+        scale = jnp.where(lat == i, quad[wave * LATS + i] / math.sqrt(NLON), scale)
+    wide = jnp.concatenate([weight[...], jnp.zeros((16, 112), F32)], axis=1)
+    taps_of[...] = jnp.concatenate([wide, jnp.zeros((112, 128), F32)], axis=0).T[0:16]
     row_odd = (lax.broadcasted_iota(jnp.int32, (80, Q2), 0) & 1) == 1
     for f in range(FIELDS):
         for i in range(LATS):
@@ -533,13 +509,34 @@
                 down = jnp.concatenate([x[79:], x[:79]], axis=0)
                 ext[RIM + LATS + k, f] = jnp.where(row_odd, down, up)
 
-    def shift_row(n, _):
-        x = ext[n // FIELDS, lax.rem(n, FIELDS)]
-        for c in range(7):
-            moved[c, n // FIELDS, lax.rem(n, FIELDS)] = shifted(x, c - 3, lane)
+    def shift_row(r, _):
+        for f in range(FIELDS):
+            x = ext[r, f]
+            moved[3, r, f] = x
+            up = jnp.concatenate([x[2:], x[:2]], axis=0)
+            down = jnp.concatenate([x[78:], x[:78]], axis=0)
+            both = jnp.concatenate([x, up, down], axis=1).astype(BF16)
+            ahead = jnp.dot(both[:, 0:256], shifts[...], preferred_element_type=F32)
+            behind = jnp.dot(
+                jnp.concatenate([both[:, 0:128], both[:, 256:384]], axis=1),
+                shifts2[...],
+                preferred_element_type=F32,
+            )
+            for c in range(3):
+                moved[4 + c, r, f] = ahead[:, 128 * c : 128 * c + 128]
+                moved[c, r, f] = behind[:, 128 * c : 128 * c + 128]
         return 0
 
-    lax.fori_loop(0, (LATS + 2 * RIM) * FIELDS, shift_row, 0)
+    rowi = lax.broadcasted_iota(jnp.int32, (256, 384), 0)
+    coli = lax.broadcasted_iota(jnp.int32, (256, 384), 1)
+    by = coli // 128 + 1
+    want = (coli & 127) + by
+    shifts[...] = jnp.where(rowi == want, 1.0, 0.0).astype(BF16)
+    by = coli // 128 - 3
+    want = (coli & 127) + by
+    want = jnp.where(want < 0, want + 256, want)
+    shifts2[...] = jnp.where(rowi == want, 1.0, 0.0).astype(BF16)
+    lax.fori_loop(0, LATS + 2 * RIM, shift_row, 0, unroll=11)
 
     def chunk(n, _):
         i, start = n // 10, pl.multiple_of(lax.rem(n, 10) * 8, 8)
@@ -547,7 +544,7 @@
         e = code[pl.ds(at, 8), :]
         t = pick[pl.ds(at, 8), :]
         taps = [
-            jnp.take_along_axis(jnp.broadcast_to(weight[k : k + 1, :], (8, 128)), t, axis=1)
+            jnp.take_along_axis(jnp.broadcast_to(taps_of[k : k + 1, :], (8, 128)), t, axis=1)
             for k in range(16)
         ]
         x0, x1 = (e & 1) == 1, (e & 2) == 2
@@ -564,7 +561,7 @@
             summed[i, f, pl.ds(start, 8), :] = total[f]
         return 0
 
-    lax.fori_loop(0, 50, chunk, 0)
+    lax.fori_loop(0, 50, chunk, 0, unroll=10)
     for n in range(LATS * FIELDS):
         i, f = n // FIELDS, n % FIELDS
         value = summed[i, f].astype(BF16)
@@ -578,13 +575,13 @@
             [mixed[pl.ds(m1, 40, stride=M1), :], mixed[pl.ds(1600 + m1, 40, stride=M1), :]], axis=1
         ).astype(BF16)
         part = lax.dot_general(phase[64 * m1 : 64 * m1 + 64, :], right, NT, preferred_element_type=F32)
-        part = (part * quad[:, 0:40]).astype(BF16)
+        part = (part * scale).astype(BF16)
         low, high = pl.ds(P2 * m1, P2), pl.ds(P2 * (M1 - 1 - m1), P2)
         for k, where in enumerate((low, low, high, high)):
             by_pair[where, 128 * k : 128 * k + 40] = part[16 * k : 16 * k + 16]
     ordered = jnp.dot(by_pair[...], sel_back[...], preferred_element_type=F32).astype(BF16)
     column = lax.broadcasted_iota(jnp.int32, (640, 640), 1)
-    onehot = jnp.where(column == place[...], 1.0, 0.0).astype(BF16)
+    onehot = jnp.where(column == order_of(place[...]), 1.0, 0.0).astype(BF16)
     slots = jnp.dot(onehot, ordered, preferred_element_type=F32)
     back[...] = jnp.concatenate(
         [slots[:, 0:128].reshape(80, 8, 128), slots[:, 128:256].reshape(80, 8, 128)], axis=1
@@ -592,13 +589,14 @@
 
 
 def stencil(rank, grid, code, pick, weight, quad, place, phase, dft_back, sel_back):
+    smem = pl.BlockSpec(memory_space=pltpu.SMEM)
     return pl.pallas_call(
         stencil_kernel,
         out_shape=(
             jax.ShapeDtypeStruct((FIELDS, 2 * LATS * Q1, Q2), BF16),
             jax.ShapeDtypeStruct((WAVES, GROUPS, 16, 128), BF16),
         ),
-        in_specs=[pl.BlockSpec(memory_space=pltpu.SMEM)] + whole(9),
+        in_specs=[smem] + whole(4) + [smem] + whole(4),
         out_specs=tuple(whole(2)),
         scratch_shapes=[
             pltpu.VMEM((LATS + 2 * RIM, FIELDS, 80, Q2), F32),
@@ -606,6 +604,9 @@
             pltpu.VMEM((LATS, FIELDS, 80, Q2), F32),
             pltpu.VMEM((3200, 128), F32),
             pltpu.VMEM((640, 512), BF16),
+            pltpu.VMEM((16, 128), F32),
+            pltpu.VMEM((256, 384), BF16),
+            pltpu.VMEM((256, 384), BF16),
         ],
         compiler_params=pltpu.CompilerParams(vmem_limit_bytes=VMEM_LIMIT),
     )(rank, grid, code, pick, weight, quad, place, phase, dft_back, sel_back)
@@ -621,20 +622,14 @@
     phase, dft, dft_back, sel, sel_back = [jnp.asarray(t) for t in phase_tables()]
     wave_rank = lax.axis_index("wave")
     band_rank = lax.axis_index("band")
-    pairs = lax.dynamic_slice_in_dim(slot_pair, wave_rank * SLOTS, SLOTS)
-    place = (slot_pair % M1) * P2 + slot_pair // M1
+    pairs = slot_pair
     rank = (band_rank * WAVES + wave_rank).reshape(1)
-    my_weight = lax.dynamic_slice_in_dim(quad_weight, wave_rank * LATS, LATS)
-    quad = jnp.repeat(my_weight / math.sqrt(NLON), 2 * FIELDS)
-    quad = jnp.pad(quad, (0, 128 - quad.shape[0])).reshape(1, 128)
-    weight = jnp.pad(stencil_weight.T, ((0, 0), (0, 112)))
-
     own = spectral.transpose(0, 2, 1).reshape(8 * SLOTS, ROWS)
     four = forward(pairs, own, legendre)
-    grid = to_grid(place.reshape(1, -1), four, phase, dft, sel)
+    grid = to_grid(slot_pair.reshape(1, -1), four, phase, dft, sel)
     arrival, back = stencil(
-        rank, grid, grid_view(depart_code), grid_view(stencil_pick), weight, quad,
-        place.reshape(-1, 1), phase, dft_back, sel_back,
+        rank, grid, grid_view(depart_code), grid_view(stencil_pick), stencil_weight, quad_weight,
+        slot_pair.reshape(-1, 1), phase, dft_back, sel_back,
     )
     total = backward(pairs, back, legendre)
     spectral_out = total.reshape(SLOTS, 8, 128)[:, :, :ROWS].transpose(0, 2, 1)

time: 115 us -> 87.8 us (0.76)
  the two profiles are of different devices: /device:TPU:8 before, /device:TPU:1 now
where the time goes in v3:
time: 87.8 us; the launch traced here: 87.3 us
  Pallas kernels  83.2 us (95%)
  local copies, waits for them, and re-layouts  3.24 us (4%)
    pallas_call x1, Pallas kernels, backward(): pl.pallas_call(backward_kernel, out_shape=jax.ShapeDtypeStruct((8 * SLOTS...  33.7 us
    pallas_call x1, Pallas kernels, forward(): pl.pallas_call(forward_kernel, out_shape=jax.ShapeDtypeStruct((WAVES, GRO...  33.2 us
    pallas_call x1, Pallas kernels, stencil(): pl.pallas_call(stencil_kernel, out_shape=(jax.ShapeDtypeStruct((FIELDS, 2...  9.45 us
    pallas_call x1, Pallas kernels, to_grid(): pl.pallas_call(to_grid_kernel, out_shape=jax.ShapeDtypeStruct((LATS + 2 *...  6.86 us

profile of v3, /device:TPU:1, one launch (start us, length us, event | category | flops | bytes accessed | tf_op | source)
XLA Modules:
  0.0 87.3 jit_solution(16784079996878960254)
XLA Ops:
  0.6 0.0 copy-start
  0.6 0.0 copy-start.2
  0.7 0.0 copy-start.1
  0.7 0.0 copy-start.4
  0.7 0.0 copy-start.3
  0.7 0.8 reshape.38.place
  1.5 0.9 %copy-done.5 = bf16[40,88,8]{1,2,0:T(8,128)(2,1)S(1)} copy-done((bf16[40,88,8]{1,2,0:T(8,128)(2,1)S(1)}, bf16[40,88,8]{1,2,0:T(8,128)(2,1)}, u32[]{:S(2)}) %copy-start.5) | copy-done | bytes 56344
  2.4 0.7 copy-done.6
  3.1 0.0 copy-start.11
  3.1 33.2 %shard_map.131.four = bf16[16,5,16,128]{3,2,1,0:T(8,128)(2,1)S(1)} custom-call(s32[640]{0:T(1024)S(1)} %copy-done.6, bf16[320,88]{1,0:T(8,128)(2,1)S(1)} %bitcast.25, bf16[40,80,1408]{2,1,0:T(8,128)(2,1)} %leg_hbm.3), custom_call_target="tpu_custom_call" | custom-call | tf_op jit(solution)/shard_map/pallas_call | solution.py:232
  36.4 0.0 copy-done.7
  36.4 0.1 reshape.48.place
  36.5 0.0 copy-done
  36.5 0.0 copy-done.2
  36.6 0.0 copy-done.9
  36.6 6.9 %shard_map.132.grid = bf16[11,4,80,128]{3,2,1,0:T(8,128)(2,1)S(1)} custom-call(s32[1,640]{1,0:T(1,128)S(1)} %reshape.38.place, bf16[16,5,16,128]{3,2,1,0:T(8,128)(2,1)S(1)} %shard_map.131.four, bf16[2560,256]{1,0:T(8,128)(2,1)S(1)} %copy-done, bf16[80,160]{1,0:T(8,128)(2,1)S(1)} %copy-done.9, bf16[256,512]{1,0:T(8,128)(2,1)S(1)} %copy-done.2), custom_call_target="tpu_custom_call" | custom-call | tf_op jit(solution)/shard_map/pallas_call | solution.py:450
  43.4 0.0 copy-done.1
  43.4 0.0 copy-done.4
  43.4 0.0 copy-done.3
  43.5 0.0 copy-done.8
  43.5 0.0 copy-done.10
  43.5 9.5 %shard_map.133 = (bf16[4,400,128]{2,1,0:T(8,128)(2,1)}, bf16[16,5,16,128]{3,2,1,0:T(8,128)(2,1)S(1)}) custom-call(s32[1]{0:T(128)} %bitcast.rank, bf16[11,4,80,128]{3,2,1,0:T(8,128)(2,1)S(1)} %shard_map.132.grid, s32[400,128]{1,0:T(8,128)S(1)} %bitcast.23, s32[400,128]{1,0:T(8,128)S(1)} %bitcast.24, f32[16,16]{1,0:T(8,128)S(1)} %copy-done.10, ...), custom_call_target="tpu_custom_call" | custom-call | tf_op jit(solution)/shard_map/pallas_call | solution.py:593
  52.9 33.7 %shard_map.134 = bf16[320,128]{1,0:T(8,128)(2,1)S(1)} custom-call(s32[640]{0:T(1024)S(1)} %copy-done.7, bf16[16,5,16,128]{3,2,1,0:T(8,128)(2,1)S(1)} %get-tuple-element.5.coef, bf16[40,80,1408]{2,1,0:T(8,128)(2,1)} %leg_hbm.3), custom_call_target="tpu_custom_call" | custom-call | tf_op jit(solution)/shard_map/pallas_call | solution.py:366
  86.6 0.6 slice_bitcast_fusion
  (7 shorter events, 0.0 us)
Async XLA Ops:
  0.6 35.9 %copy-start = (bf16[2560,256]{1,0:T(8,128)(2,1)S(1)}, bf16[2560,256]{1,0:T(8,128)(2,1)}, u32[]{:S(2)}) copy-start(bf16[2560,256]{1,0:T(8,128)(2,1)} %constant.19.clone.phase) | copy-start | bytes 3932164
  0.6 35.9 %copy-start.2 = (bf16[256,512]{1,0:T(8,128)(2,1)S(1)}, bf16[256,512]{1,0:T(8,128)(2,1)}, u32[]{:S(2)}) copy-start(bf16[256,512]{1,0:T(8,128)(2,1)} %constant.22.clone.sel) | copy-start | bytes 786436
  0.7 42.8 %copy-start.1 = (bf16[512,256]{1,0:T(8,128)(2,1)S(1)}, bf16[512,256]{1,0:T(8,128)(2,1)}, u32[]{:S(2)}) copy-start(bf16[512,256]{1,0:T(8,128)(2,1)} %constant.23.clone.sel_back) | copy-start | bytes 786436
  0.7 42.8 %copy-start.4 = (s32[1,2,5,5120]{3,1,2,0:T(2,128)S(1)}, s32[1,2,5,5120]{3,1,2,0:T(2,128)}, u32[]{:S(2)}) copy-start(s32[1,2,5,5120]{3,1,2,0:T(2,128)} %param.17) | copy-start | bytes 614404
  0.7 42.8 %copy-start.3 = (s32[1,2,5,5120]{3,1,2,0:T(2,128)S(1)}, s32[1,2,5,5120]{3,1,2,0:T(2,128)}, u32[]{:S(2)}) copy-start(s32[1,2,5,5120]{3,1,2,0:T(2,128)} %param.16) | copy-start | bytes 614404
  1.5 0.9 %copy-start.5 = (bf16[40,88,8]{1,2,0:T(8,128)(2,1)S(1)}, bf16[40,88,8]{1,2,0:T(8,128)(2,1)}, u32[]{:S(2)}) copy-start(bf16[40,88,8]{1,2,0:T(8,128)(2,1)} %param.12) | copy-start | bytes 168964
  2.4 0.7 copy-start.6
  3.1 33.3 %copy-start.7 = (s32[640]{0:T(1024)S(1)}, s32[640]{0:T(1024)}, u32[]{:S(2)}) copy-start(s32[640]{0:T(1024)} %pairs.3) | copy-start | bytes 7684
  3.1 33.4 %copy-start.9 = (bf16[80,160]{1,0:T(8,128)(2,1)S(1)}, bf16[80,160]{1,0:T(8,128)(2,1)}, u32[]{:S(2)}) copy-start(bf16[80,160]{1,0:T(8,128)(2,1)} %constant.20.clone.dft) | copy-start | bytes 76804
  3.1 40.3 %copy-start.8 = (bf16[160,80]{1,0:T(8,128)(2,1)S(1)}, bf16[160,80]{1,0:T(8,128)(2,1)}, u32[]{:S(2)}) copy-start(bf16[160,80]{1,0:T(8,128)(2,1)} %constant.21.clone.dft_back) | copy-start | bytes 76804
  3.1 40.4 %copy-start.10 = (f32[16,16]{1,0:T(8,128)S(1)}, f32[16,16]{1,0:T(8,128)}, u32[]{:S(2)}) copy-start(f32[16,16]{1,0:T(8,128)} %weight.1) | copy-start | bytes 3076
  3.1 40.4 %copy-start.11 = (f32[80]{0:T(128)S(1)}, f32[80]{0:T(128)}, u32[]{:S(2)}) copy-start(f32[80]{0:T(128)} %quad.1) | copy-start | bytes 964

commit v4 on v3

--- a/solution.py
+++ b/solution.py
@@ -69,6 +69,7 @@
 GROUP = SLOTS // GROUPS
 TALL = 8 * GROUP
 HALF = TALL // 2
+WIDE = 384
 STEPS = (1, 3, 2)
 SIDE = 4
 
@@ -96,6 +97,10 @@
     def along_v(self, by):
         v = turn(self.v, by)
         return {"band": self.u * SIDE + v if self.x_first else v * SIDE + self.u}
+
+
+def side_by_side(pieces):
+    return jnp.concatenate(pieces + [jnp.zeros((8, WIDE - 4 * ROWS), F32)], axis=1).astype(BF16)
 
 
 def turn(at, by):
@@ -135,11 +140,14 @@
 
 
 def forward_kernel(
-    pairs, spec, leg_hbm, out,
-    leg, gath, rows, held, packed, leg_sem, plane_send, plane_recv, wave_send, wave_recv,
+    pairs, spec_hbm, leg_hbm, out,
+    spec, leg, gath, rows, held, packed, leg_sem, spec_sem, plane_send, plane_recv, wave_send, wave_recv,
 ):
     me = lax.axis_index("wave")
+    spec_load = pltpu.make_async_copy(spec_hbm, spec, spec_sem)
+    spec_load.start()
     barrier, greeted = greet()
+    spec_load.wait()
     loads = [
         pltpu.make_async_copy(
             leg_hbm.at[pl.ds(GROUP * g, GROUP)], leg.at[pl.ds(GROUP * g, GROUP)], leg_sem.at[g]
@@ -151,9 +159,8 @@
         for k in range(2):
             p = Plane(k)
             start = TALL * g + HALF * k
-            own = jnp.concatenate(
-                [spec[start : start + HALF, :], jnp.zeros((HALF, 128 - ROWS), BF16)], axis=1
-            )
+            own = spec[start : start + HALF, :].astype(F32)
+            own = side_by_side([own[8 * m : 8 * m + 8] for m in range(4)])
             if k == 0:
                 gath[g, 0, p.u, p.v] = own
                 one, line = gath.at[g, 0, p.u, p.v], gath.at[g, 0, :, p.v]
@@ -180,9 +187,10 @@
     def multiply(g):
         for b in range(BANDS):
             for k in range(2):
-                rows[HALF * k : HALF * (k + 1), ROWS * b : ROWS * (b + 1)] = gath[
-                    g, k, b // SIDE, b % SIDE
-                ].astype(F32)[:, :ROWS]
+                block = gath[g, k, b // SIDE, b % SIDE].astype(F32)
+                for m in range(4):
+                    at = HALF * k + 8 * m
+                    rows[at : at + 8, ROWS * b : ROWS * (b + 1)] = block[:, ROWS * m : ROWS * (m + 1)]
 
         def slots(part, _):
             for k in range(4):
@@ -234,17 +242,19 @@
         out_shape=jax.ShapeDtypeStruct((WAVES, GROUPS, 16, 128), BF16),
         in_specs=[
             pl.BlockSpec(memory_space=pltpu.SMEM),
-            pl.BlockSpec(memory_space=pltpu.VMEM),
+            pl.BlockSpec(memory_space=pl.ANY),
             pl.BlockSpec(memory_space=pl.ANY),
         ],
         out_specs=pl.BlockSpec(memory_space=pltpu.VMEM),
         scratch_shapes=[
+            pltpu.VMEM((8 * SLOTS, ROWS), BF16),
             pltpu.VMEM((SLOTS, BAND_LATS, NROW), BF16),
-            pltpu.VMEM((GROUPS, 2, SIDE, SIDE, HALF, 128), BF16),
+            pltpu.VMEM((GROUPS, 2, SIDE, SIDE, 8, WIDE), BF16),
             pltpu.VMEM((TALL, NROW), F32),
             pltpu.VMEM((GROUP * BAND_LATS, 128), F32),
             pltpu.VMEM((WAVES, GROUPS, 16, 128), BF16),
             pltpu.SemaphoreType.DMA((GROUPS,)),
+            pltpu.SemaphoreType.DMA,
             pltpu.SemaphoreType.DMA((GROUPS, 2, 6)),
             pltpu.SemaphoreType.DMA((GROUPS, 2, 6)),
             pltpu.SemaphoreType.DMA((GROUPS, WAVES)),
@@ -319,42 +329,46 @@
 
         lax.fori_loop(0, GROUP // 4, slots, 0)
         for b in range(BANDS):
-            both = jnp.concatenate(
-                [tall[:, ROWS * b : ROWS * (b + 1)], jnp.zeros((TALL, 128 - ROWS), F32)], axis=1
-            ).astype(BF16)
             for k in range(2):
-                part[g, k, b // SIDE, b % SIDE] = both[HALF * k : HALF * (k + 1)]
-
-    for t in range(GROUPS + 2):
-        g = t
-        if 0 <= g < GROUPS:
-            for copy in waves[g]:
-                copy.wait_recv()
-            loads[g].wait()
-            multiply(g)
-            for k in range(6):
-                near[6 * g + k].start()
-        g = t - 1
-        if 0 <= g < GROUPS:
-            for k in range(2):
-                p = Plane(k)
-                total = (part[g, 0, p.u] if k == 0 else part[g, 1, :, p.u]).astype(F32)
-                for n in range(3):
-                    near[6 * g + 3 * k + n].wait_recv()
-                    total = total + first[g, k, n].astype(F32)
-                line[g, k] = total
-                line_out[g, k] = total.astype(BF16)
-                for n in range(3):
-                    far[6 * g + 3 * k + n].start()
-        g = t - 2
-        if 0 <= g < GROUPS:
-            for k in range(2):
-                total = line[g, k, Plane(k).v]
-                for n in range(3):
-                    far[6 * g + 3 * k + n].wait_recv()
-                    total = total + second[g, k, n].astype(F32)
-                start = TALL * g + HALF * k
-                out[start : start + HALF, :] = total.astype(BF16)
+                part[g, k, b // SIDE, b % SIDE] = side_by_side(
+                    [
+                        tall[HALF * k + 8 * m : HALF * k + 8 * m + 8, ROWS * b : ROWS * (b + 1)]
+                        for m in range(4)
+                    ]
+                )
+
+    for g in range(GROUPS):
+        for copy in waves[g]:
+            copy.wait_recv()
+        loads[g].wait()
+        multiply(g)
+        for k in range(6):
+            near[6 * g + k].start()
+    for g in range(GROUPS):
+        for k in range(2):
+            p = Plane(k)
+            total = (part[g, 0, p.u] if k == 0 else part[g, 1, :, p.u]).astype(F32)
+            for n in range(3):
+                near[6 * g + 3 * k + n].wait_recv()
+                total = total + first[g, k, n].astype(F32)
+            line[g, k] = total
+            line_out[g, k] = total.astype(BF16)
+            for n in range(3):
+                far[6 * g + 3 * k + n].start()
+    for g in range(GROUPS):
+        for k in range(2):
+            total = line[g, k, Plane(k).v]
+            for n in range(3):
+                far[6 * g + 3 * k + n].wait_recv()
+                total = total + second[g, k, n].astype(F32)
+            start = TALL * g + HALF * k
+            pieces = [
+                jnp.concatenate(
+                    [total[:, ROWS * m : ROWS * (m + 1)], jnp.zeros((8, 128 - ROWS), F32)], axis=1
+                )
+                for m in range(4)
+            ]
+            out[start : start + HALF, :] = jnp.concatenate(pieces, axis=0).astype(BF16)
     for hop in near + far:
         hop.wait_send()
     for copies in waves:
@@ -377,11 +391,11 @@
             pltpu.VMEM((WAVES, GROUPS, 16, 128), BF16),
             pltpu.VMEM((GROUP * BAND_LATS, 128), F32),
             pltpu.VMEM((TALL, NROW), F32),
-            pltpu.VMEM((GROUPS, 2, SIDE, SIDE, HALF, 128), BF16),
-            pltpu.VMEM((GROUPS, 2, 3, SIDE, HALF, 128), BF16),
-            pltpu.VMEM((GROUPS, 2, SIDE, HALF, 128), F32),
-            pltpu.VMEM((GROUPS, 2, SIDE, HALF, 128), BF16),
-            pltpu.VMEM((GROUPS, 2, 3, HALF, 128), BF16),
+            pltpu.VMEM((GROUPS, 2, SIDE, SIDE, 8, WIDE), BF16),
+            pltpu.VMEM((GROUPS, 2, 3, SIDE, 8, WIDE), BF16),
+            pltpu.VMEM((GROUPS, 2, SIDE, 8, WIDE), F32),
+            pltpu.VMEM((GROUPS, 2, SIDE, 8, WIDE), BF16),
+            pltpu.VMEM((GROUPS, 2, 3, 8, WIDE), BF16),
             pltpu.SemaphoreType.DMA((GROUPS,)),
             pltpu.SemaphoreType.DMA((GROUPS, WAVES)),
             pltpu.SemaphoreType.DMA((GROUPS, WAVES)),
@@ -403,7 +417,7 @@
     for where in ids:
         pl.semaphore_signal(barrier, inc=1, device_id=where, device_id_type=MESH)
     row = lax.broadcasted_iota(jnp.int32, (640, 640), 0)
-    onehot = jnp.where(row == order_of(place[...]), 1.0, 0.0).astype(BF16)
+    onehot = jnp.where(row == order_of(place[...].reshape(1, 640)), 1.0, 0.0).astype(BF16)
     blocks = four[...].astype(F32)
     slots = jnp.concatenate(
         [blocks[:, :, 0:8].reshape(640, 128), blocks[:, :, 8:16].reshape(640, 128)], axis=1
@@ -580,9 +594,9 @@
         for k, where in enumerate((low, low, high, high)):
             by_pair[where, 128 * k : 128 * k + 40] = part[16 * k : 16 * k + 16]
     ordered = jnp.dot(by_pair[...], sel_back[...], preferred_element_type=F32).astype(BF16)
-    column = lax.broadcasted_iota(jnp.int32, (640, 640), 1)
-    onehot = jnp.where(column == order_of(place[...]), 1.0, 0.0).astype(BF16)
-    slots = jnp.dot(onehot, ordered, preferred_element_type=F32)
+    row = lax.broadcasted_iota(jnp.int32, (640, 640), 0)
+    onehot = jnp.where(row == order_of(place[...].reshape(1, 640)), 1.0, 0.0).astype(BF16)
+    slots = lax.dot_general(onehot, ordered, TN, preferred_element_type=F32)
     back[...] = jnp.concatenate(
         [slots[:, 0:128].reshape(80, 8, 128), slots[:, 128:256].reshape(80, 8, 128)], axis=1
     ).astype(BF16).reshape(WAVES, GROUPS, 16, 128)
@@ -626,10 +640,10 @@
     rank = (band_rank * WAVES + wave_rank).reshape(1)
     own = spectral.transpose(0, 2, 1).reshape(8 * SLOTS, ROWS)
     four = forward(pairs, own, legendre)
-    grid = to_grid(slot_pair.reshape(1, -1), four, phase, dft, sel)
+    grid = to_grid(slot_pair, four, phase, dft, sel)
     arrival, back = stencil(
         rank, grid, grid_view(depart_code), grid_view(stencil_pick), stencil_weight, quad_weight,
-        slot_pair.reshape(-1, 1), phase, dft_back, sel_back,
+        slot_pair, phase, dft_back, sel_back,
     )
     total = backward(pairs, back, legendre)
     spectral_out = total.reshape(SLOTS, 8, 128)[:, :, :ROWS].transpose(0, 2, 1)

time: 87.8 us -> 81.7 us (0.931)
  Pallas kernels: 83.2 us -> 78.3 us
    pallas_call x1, Pallas kernels: 33.7 us -> 29.5 us  [backward(): pl.pallas_call(backward_kernel, out_shape=jax.ShapeDtypeStruct((8 * SLOTS...]
    reshape x2 -> x0, local copies, waits for them, and re-layouts: 0.98 us -> none  [the longest x1 0.84 us: per_device(): grid = to_grid(slot_pair.reshape(1, -1), four, phase, dft, sel)]
    unnamed x24 -> x22, local copies, waits for them, and re-layouts: 1.62 us -> 1.76 us
where the time goes in v4:
time: 81.7 us; the launch traced here: 81.5 us
  Pallas kernels  78.3 us (96%)
  local copies, waits for them, and re-layouts  2.4 us (3%)
    pallas_call x1, Pallas kernels, forward(): pl.pallas_call(forward_kernel, out_shape=jax.ShapeDtypeStruct((WAVES, GRO...  32.7 us
    pallas_call x1, Pallas kernels, backward(): pl.pallas_call(backward_kernel, out_shape=jax.ShapeDtypeStruct((8 * SLOTS...  29.5 us
    pallas_call x1, Pallas kernels, stencil(): pl.pallas_call(stencil_kernel, out_shape=(jax.ShapeDtypeStruct((FIELDS, 2...  9.42 us
    pallas_call x1, Pallas kernels, to_grid(): pl.pallas_call(to_grid_kernel, out_shape=jax.ShapeDtypeStruct((LATS + 2 *...  6.71 us
    unnamed x22, local copies, waits for them, and re-layouts  1.76 us

profile of v4, /device:TPU:1, one launch (start us, length us, event | category | flops | bytes accessed | tf_op | source)
XLA Modules:
  0.0 81.5 jit_solution(9579342841173552283)
XLA Ops:
  0.6 0.0 copy-start
  0.6 0.0 copy-start.2
  0.7 0.0 copy-start.1
  0.7 0.0 copy-start.4
  0.7 0.0 copy-start.3
  0.7 0.0 copy-start.5
  0.7 1.0 %copy-done.5 = bf16[40,88,8]{1,2,0:T(8,128)(2,1)S(1)} copy-done((bf16[40,88,8]{1,2,0:T(8,128)(2,1)S(1)}, bf16[40,88,8]{1,2,0:T(8,128)(2,1)}, u32[]{:S(2)}) %copy-start.5) | copy-done | bytes 56344
  1.7 0.0 copy-start.6
  1.7 0.7 copy-done.6
  2.4 0.0 copy-start.8
  2.4 32.7 %shard_map.131.four = bf16[16,5,16,128]{3,2,1,0:T(8,128)(2,1)S(1)} custom-call(s32[640]{0:T(1024)S(1)} %copy-done.6, bf16[320,88]{1,0:T(8,128)(2,1)S(1)} %bitcast.25, bf16[40,80,1408]{2,1,0:T(8,128)(2,1)} %leg_hbm.3), custom_call_target="tpu_custom_call" | custom-call | tf_op jit(solution)/shard_map/pallas_call | solution.py:240
  35.2 0.0 copy-done
  35.2 0.0 copy-done.2
  35.2 0.0 copy-done.8
  35.2 6.7 %shard_map.132.grid = bf16[11,4,80,128]{3,2,1,0:T(8,128)(2,1)S(1)} custom-call(s32[640]{0:T(1024)S(1)} %copy-done.6, bf16[16,5,16,128]{3,2,1,0:T(8,128)(2,1)S(1)} %shard_map.131.four, bf16[2560,256]{1,0:T(8,128)(2,1)S(1)} %copy-done, bf16[80,160]{1,0:T(8,128)(2,1)S(1)} %copy-done.8, bf16[256,512]{1,0:T(8,128)(2,1)S(1)} %copy-done.2), custom_call_target="tpu_custom_call" | custom-call | tf_op jit(solution)/shard_map/pallas_call | solution.py:464
  41.9 0.0 copy-done.1
  41.9 0.0 copy-done.4
  41.9 0.0 copy-done.3
  41.9 0.0 copy-done.7
  42.0 0.0 copy-done.9
  42.0 0.0 copy-done.10
  42.0 9.4 %shard_map.133 = (bf16[4,400,128]{2,1,0:T(8,128)(2,1)}, bf16[16,5,16,128]{3,2,1,0:T(8,128)(2,1)S(1)}) custom-call(s32[1]{0:T(128)} %bitcast.rank, bf16[11,4,80,128]{3,2,1,0:T(8,128)(2,1)S(1)} %shard_map.132.grid, s32[400,128]{1,0:T(8,128)S(1)} %bitcast.23, s32[400,128]{1,0:T(8,128)S(1)} %bitcast.24, f32[16,16]{1,0:T(8,128)S(1)} %copy-done.9, ...), custom_call_target="tpu_custom_call" | custom-call | tf_op jit(solution)/shard_map/pallas_call | solution.py:607
  51.4 29.5 %shard_map.134 = bf16[320,128]{1,0:T(8,128)(2,1)S(1)} custom-call(s32[640]{0:T(1024)S(1)} %copy-done.6, bf16[16,5,16,128]{3,2,1,0:T(8,128)(2,1)S(1)} %get-tuple-element.5.coef, bf16[40,80,1408]{2,1,0:T(8,128)(2,1)} %leg_hbm.3), custom_call_target="tpu_custom_call" | custom-call | tf_op jit(solution)/shard_map/pallas_call | solution.py:380
  80.9 0.6 slice_bitcast_fusion
  (3 shorter events, 0.0 us)
Async XLA Ops:
  0.6 34.5 %copy-start = (bf16[2560,256]{1,0:T(8,128)(2,1)S(1)}, bf16[2560,256]{1,0:T(8,128)(2,1)}, u32[]{:S(2)}) copy-start(bf16[2560,256]{1,0:T(8,128)(2,1)} %constant.19.clone.phase) | copy-start | bytes 3932164
  0.6 34.5 %copy-start.2 = (bf16[256,512]{1,0:T(8,128)(2,1)S(1)}, bf16[256,512]{1,0:T(8,128)(2,1)}, u32[]{:S(2)}) copy-start(bf16[256,512]{1,0:T(8,128)(2,1)} %constant.22.clone.sel) | copy-start | bytes 786436
  0.7 41.3 %copy-start.1 = (bf16[512,256]{1,0:T(8,128)(2,1)S(1)}, bf16[512,256]{1,0:T(8,128)(2,1)}, u32[]{:S(2)}) copy-start(bf16[512,256]{1,0:T(8,128)(2,1)} %constant.23.clone.sel_back) | copy-start | bytes 786436
  0.7 41.3 %copy-start.4 = (s32[1,2,5,5120]{3,1,2,0:T(2,128)S(1)}, s32[1,2,5,5120]{3,1,2,0:T(2,128)}, u32[]{:S(2)}) copy-start(s32[1,2,5,5120]{3,1,2,0:T(2,128)} %param.17) | copy-start | bytes 614404
  0.7 41.3 %copy-start.3 = (s32[1,2,5,5120]{3,1,2,0:T(2,128)S(1)}, s32[1,2,5,5120]{3,1,2,0:T(2,128)}, u32[]{:S(2)}) copy-start(s32[1,2,5,5120]{3,1,2,0:T(2,128)} %param.16) | copy-start | bytes 614404
  0.7 1.0 %copy-start.5 = (bf16[40,88,8]{1,2,0:T(8,128)(2,1)S(1)}, bf16[40,88,8]{1,2,0:T(8,128)(2,1)}, u32[]{:S(2)}) copy-start(bf16[40,88,8]{1,2,0:T(8,128)(2,1)} %param.12) | copy-start | bytes 168964
  1.7 0.7 copy-start.6
  2.4 32.8 %copy-start.8 = (bf16[80,160]{1,0:T(8,128)(2,1)S(1)}, bf16[80,160]{1,0:T(8,128)(2,1)}, u32[]{:S(2)}) copy-start(bf16[80,160]{1,0:T(8,128)(2,1)} %constant.20.clone.dft) | copy-start | bytes 76804
  2.4 39.5 %copy-start.7 = (bf16[160,80]{1,0:T(8,128)(2,1)S(1)}, bf16[160,80]{1,0:T(8,128)(2,1)}, u32[]{:S(2)}) copy-start(bf16[160,80]{1,0:T(8,128)(2,1)} %constant.21.clone.dft_back) | copy-start | bytes 76804
  2.4 39.5 %copy-start.9 = (f32[16,16]{1,0:T(8,128)S(1)}, f32[16,16]{1,0:T(8,128)}, u32[]{:S(2)}) copy-start(f32[16,16]{1,0:T(8,128)} %weight.1) | copy-start | bytes 3076
  2.4 39.5 %copy-start.10 = (f32[80]{0:T(128)S(1)}, f32[80]{0:T(128)}, u32[]{:S(2)}) copy-start(f32[80]{0:T(128)} %quad.1) | copy-start | bytes 964

commit v5 on v4

--- a/solution.py
+++ b/solution.py
@@ -131,7 +131,7 @@
 def wave_copies(src, dst, g, send_sem, recv_sem):
     me = lax.axis_index("wave")
     copies = []
-    for d in range(1, WAVES):
+    for d in sorted(range(1, WAVES), key=lambda d: (abs(d - WAVES // 2), d)):
         peer = lax.rem(me + d, WAVES)
         copies.append(
             remote(src.at[peer, g], dst.at[me, g], send_sem.at[g, d], recv_sem.at[g, d], {"wave": peer})
@@ -208,7 +208,7 @@
                 )
             return 0
 
-        lax.fori_loop(0, GROUP // 4, slots, 0)
+        lax.fori_loop(0, GROUP // 4, slots, 0, unroll=2)
         for w in range(WAVES):
             part = [held[pl.ds(LATS * w + i, GROUP, stride=BAND_LATS), :][:, 0:32] for i in range(LATS)]
             first = jnp.concatenate(part[:4], axis=1)
@@ -327,7 +327,7 @@
                 tall[pl.ds(pl.multiple_of(8 * at, 8), 8), :] = jnp.where(higher, high, low) * used
             return 0
 
-        lax.fori_loop(0, GROUP // 4, slots, 0)
+        lax.fori_loop(0, GROUP // 4, slots, 0, unroll=2)
         for b in range(BANDS):
             for k in range(2):
                 part[g, k, b // SIDE, b % SIDE] = side_by_side(

time: 81.7 us -> 78.9 us (0.966)
  Pallas kernels: 78.3 us -> 75.6 us
    pallas_call x1, Pallas kernels: 29.5 us -> 27.7 us  [backward(): pl.pallas_call(backward_kernel, out_shape=jax.ShapeDtypeStruct((8 * SLOTS...]
    pallas_call x1, Pallas kernels: 32.7 us -> 31.4 us  [forward(): pl.pallas_call(forward_kernel, out_shape=jax.ShapeDtypeStruct((WAVES, GRO...]
where the time goes in v5:
time: 78.9 us; the launch traced here: 78.8 us
  Pallas kernels  75.6 us (96%)
  local copies, waits for them, and re-layouts  2.4 us (3%)
  between operations  0.79 us (1%)
    pallas_call x1, Pallas kernels, forward(): pl.pallas_call(forward_kernel, out_shape=jax.ShapeDtypeStruct((WAVES, GRO...  31.4 us
    pallas_call x1, Pallas kernels, backward(): pl.pallas_call(backward_kernel, out_shape=jax.ShapeDtypeStruct((8 * SLOTS...  27.7 us
    pallas_call x1, Pallas kernels, stencil(): pl.pallas_call(stencil_kernel, out_shape=(jax.ShapeDtypeStruct((FIELDS, 2...  9.42 us
    pallas_call x1, Pallas kernels, to_grid(): pl.pallas_call(to_grid_kernel, out_shape=jax.ShapeDtypeStruct((LATS + 2 *...  7.13 us
    unnamed x22, local copies, waits for them, and re-layouts  1.76 us

profile of v5, /device:TPU:1, one launch (start us, length us, event | category | flops | bytes accessed | tf_op | source)
XLA Modules:
  0.0 78.8 jit_solution(8053409586433180066)
XLA Ops:
  0.6 0.0 copy-start
  0.6 0.0 copy-start.2
  0.7 0.0 copy-start.1
  0.7 0.0 copy-start.4
  0.7 0.0 copy-start.3
  0.7 0.0 copy-start.5
  0.7 1.0 %copy-done.5 = bf16[40,88,8]{1,2,0:T(8,128)(2,1)S(1)} copy-done((bf16[40,88,8]{1,2,0:T(8,128)(2,1)S(1)}, bf16[40,88,8]{1,2,0:T(8,128)(2,1)}, u32[]{:S(2)}) %copy-start.5) | copy-done | bytes 56344
  1.7 0.0 copy-start.6
  1.7 0.7 copy-done.6
  2.4 0.0 copy-start.8
  2.4 31.4 %shard_map.131.four = bf16[16,5,16,128]{3,2,1,0:T(8,128)(2,1)S(1)} custom-call(s32[640]{0:T(1024)S(1)} %copy-done.6, bf16[320,88]{1,0:T(8,128)(2,1)S(1)} %bitcast.25, bf16[40,80,1408]{2,1,0:T(8,128)(2,1)} %leg_hbm.3), custom_call_target="tpu_custom_call" | custom-call | tf_op jit(solution)/shard_map/pallas_call | solution.py:240
  33.8 0.0 copy-done
  33.8 0.0 copy-done.2
  33.8 0.0 copy-done.8
  33.8 7.1 %shard_map.132.grid = bf16[11,4,80,128]{3,2,1,0:T(8,128)(2,1)S(1)} custom-call(s32[640]{0:T(1024)S(1)} %copy-done.6, bf16[16,5,16,128]{3,2,1,0:T(8,128)(2,1)S(1)} %shard_map.131.four, bf16[2560,256]{1,0:T(8,128)(2,1)S(1)} %copy-done, bf16[80,160]{1,0:T(8,128)(2,1)S(1)} %copy-done.8, bf16[256,512]{1,0:T(8,128)(2,1)S(1)} %copy-done.2), custom_call_target="tpu_custom_call" | custom-call | tf_op jit(solution)/shard_map/pallas_call | solution.py:464
  41.0 0.0 copy-done.1
  41.0 0.0 copy-done.4
  41.0 0.0 copy-done.3
  41.0 0.0 copy-done.7
  41.0 0.0 copy-done.9
  41.0 0.0 copy-done.10
  41.0 9.4 %shard_map.133 = (bf16[4,400,128]{2,1,0:T(8,128)(2,1)}, bf16[16,5,16,128]{3,2,1,0:T(8,128)(2,1)S(1)}) custom-call(s32[1]{0:T(128)} %bitcast.rank, bf16[11,4,80,128]{3,2,1,0:T(8,128)(2,1)S(1)} %shard_map.132.grid, s32[400,128]{1,0:T(8,128)S(1)} %bitcast.23, s32[400,128]{1,0:T(8,128)S(1)} %bitcast.24, f32[16,16]{1,0:T(8,128)S(1)} %copy-done.9, ...), custom_call_target="tpu_custom_call" | custom-call | tf_op jit(solution)/shard_map/pallas_call | solution.py:607
  50.4 27.7 %shard_map.134 = bf16[320,128]{1,0:T(8,128)(2,1)S(1)} custom-call(s32[640]{0:T(1024)S(1)} %copy-done.6, bf16[16,5,16,128]{3,2,1,0:T(8,128)(2,1)S(1)} %get-tuple-element.5.coef, bf16[40,80,1408]{2,1,0:T(8,128)(2,1)} %leg_hbm.3), custom_call_target="tpu_custom_call" | custom-call | tf_op jit(solution)/shard_map/pallas_call | solution.py:380
  78.2 0.6 slice_bitcast_fusion
  (3 shorter events, 0.0 us)
Async XLA Ops:
  0.6 33.2 %copy-start = (bf16[2560,256]{1,0:T(8,128)(2,1)S(1)}, bf16[2560,256]{1,0:T(8,128)(2,1)}, u32[]{:S(2)}) copy-start(bf16[2560,256]{1,0:T(8,128)(2,1)} %constant.19.clone.phase) | copy-start | bytes 3932164
  0.6 33.2 %copy-start.2 = (bf16[256,512]{1,0:T(8,128)(2,1)S(1)}, bf16[256,512]{1,0:T(8,128)(2,1)}, u32[]{:S(2)}) copy-start(bf16[256,512]{1,0:T(8,128)(2,1)} %constant.22.clone.sel) | copy-start | bytes 786436
  0.7 40.3 %copy-start.1 = (bf16[512,256]{1,0:T(8,128)(2,1)S(1)}, bf16[512,256]{1,0:T(8,128)(2,1)}, u32[]{:S(2)}) copy-start(bf16[512,256]{1,0:T(8,128)(2,1)} %constant.23.clone.sel_back) | copy-start | bytes 786436
  0.7 40.3 %copy-start.4 = (s32[1,2,5,5120]{3,1,2,0:T(2,128)S(1)}, s32[1,2,5,5120]{3,1,2,0:T(2,128)}, u32[]{:S(2)}) copy-start(s32[1,2,5,5120]{3,1,2,0:T(2,128)} %param.17) | copy-start | bytes 614404
  0.7 40.3 %copy-start.3 = (s32[1,2,5,5120]{3,1,2,0:T(2,128)S(1)}, s32[1,2,5,5120]{3,1,2,0:T(2,128)}, u32[]{:S(2)}) copy-start(s32[1,2,5,5120]{3,1,2,0:T(2,128)} %param.16) | copy-start | bytes 614404
  0.7 1.0 %copy-start.5 = (bf16[40,88,8]{1,2,0:T(8,128)(2,1)S(1)}, bf16[40,88,8]{1,2,0:T(8,128)(2,1)}, u32[]{:S(2)}) copy-start(bf16[40,88,8]{1,2,0:T(8,128)(2,1)} %param.12) | copy-start | bytes 168964
  1.7 0.7 copy-start.6
  2.4 31.4 %copy-start.8 = (bf16[80,160]{1,0:T(8,128)(2,1)S(1)}, bf16[80,160]{1,0:T(8,128)(2,1)}, u32[]{:S(2)}) copy-start(bf16[80,160]{1,0:T(8,128)(2,1)} %constant.20.clone.dft) | copy-start | bytes 76804
  2.4 38.6 %copy-start.7 = (bf16[160,80]{1,0:T(8,128)(2,1)S(1)}, bf16[160,80]{1,0:T(8,128)(2,1)}, u32[]{:S(2)}) copy-start(bf16[160,80]{1,0:T(8,128)(2,1)} %constant.21.clone.dft_back) | copy-start | bytes 76804
  2.4 38.6 %copy-start.9 = (f32[16,16]{1,0:T(8,128)S(1)}, f32[16,16]{1,0:T(8,128)}, u32[]{:S(2)}) copy-start(f32[16,16]{1,0:T(8,128)} %weight.1) | copy-start | bytes 3076
  2.4 38.6 %copy-start.10 = (f32[80]{0:T(128)S(1)}, f32[80]{0:T(128)}, u32[]{:S(2)}) copy-start(f32[80]{0:T(128)} %quad.1) | copy-start | bytes 964
